TPU v7x, 256 devices: a whole 4x4x8 slice. The times are simulated.
256 devices in a mesh: grp: 16 (over y_lo, z), sp: 16 (over y_hi, x, core).
Axes of the slice: x: 4, y: 4 (y_hi: 2, y_lo: 2; y = y_hi * 2 + y_lo), z: 8, core: 2. Of those that a mesh axis runs over, the one named last changes fastest.
Arguments:
- queries: bfloat16 [32768, 5120], P(('grp', 'sp')), may hold values from -8 to 8
- keys: bfloat16 [32768, 1024], P(('grp', 'sp')), may hold values from -8 to 8
- values: bfloat16 [32768, 1024], P(('grp', 'sp')), may hold values from -6 to 6
- slot_order: int32 [16, 16, 128], P('grp', 'sp'), may hold values from 0 to 127, each once within a row
- doc_ids: int32 [16, 2048], P('grp'), may hold values from 0 to 3, never falling along the last dimension, each value on 1 to 1024 neighbouring positions
Outputs:
- attended: bfloat16 [32768, 5120], P(('grp', 'sp'))
Inputs may be any that keep to these rules, and one draw needn't show every extreme that they name: `slot_order`: each row of the last dimension is a permutation. `doc_ids`: never falling along a group's positions; every document spans at most 1024 positions, and some document spans exactly 1024.
All inputs are finite; a program needn't handle non-finite values.
Results may differ from a plain program's by a relative error of at most 0.0027.
Values may be sent and summed in bfloat16 or wider, within the bound.
No kernel may reach another device: no remote copies, remote signals or barrier semaphores. Data moves between devices by JAX's collectives and lax.ppermute only.
A program may use at most 128 MiB of HBM per device.

v0:
```python
import jax
import jax.numpy as jnp
from jax import lax
from jax.sharding import PartitionSpec as P

QH = 40
KVH = 8
HD = 128


def passed_along(value, axis, steps):
    count = lax.axis_size(axis)
    first, last = (max(0, -steps), min(count, count - steps))
    return lax.ppermute(value, axis, [(source, source + steps) for source in range(first, last)])


def window_mask(seg_padded, member, rows_dev, max_reach):
    key_seg = lax.dynamic_slice_in_dim(seg_padded, member * rows_dev, (max_reach + 1) * rows_dev)
    query_seg = lax.dynamic_slice_in_dim(seg_padded, (member + max_reach) * rows_dev, rows_dev)
    column = jnp.arange((max_reach + 1) * rows_dev, dtype=jnp.int32)
    row_pos = jnp.arange(rows_dev, dtype=jnp.int32)
    same_doc = key_seg[None, :] == query_seg[:, None]
    return same_doc & (column[None, :] <= row_pos[:, None] + max_reach * rows_dev)


def window_attention(group_q, group_k, group_v, doc_row):
    rows_dev = group_q.shape[0]
    max_reach = min(8, lax.axis_size("sp") - 1)
    member = lax.axis_index("sp")
    kv_blocks = [None] * (max_reach + 1)
    kv_blocks[max_reach] = (group_k, group_v)
    for distance in range(1, max_reach + 1):
        kv_blocks[max_reach - distance] = passed_along((group_k, group_v), "sp", distance)
    key_win = jnp.concatenate([pair[0] for pair in kv_blocks], axis=0)
    val_win = jnp.concatenate([pair[1] for pair in kv_blocks], axis=0)
    seg_padded = jnp.concatenate([jnp.full((max_reach * rows_dev,), -1, jnp.int32), doc_row])
    allowed = window_mask(seg_padded, member, rows_dev, max_reach)
    scale = HD ** (-0.5)
    group_size = QH // KVH
    query_split = group_q.reshape(rows_dev, KVH, group_size, HD)
    head_outputs = []
    for kv_head in range(KVH):
        key_head = key_win[:, kv_head * HD : (kv_head + 1) * HD]
        val_head = val_win[:, kv_head * HD : (kv_head + 1) * HD]
        query_head = query_split[:, kv_head]
        scores = (
            jnp.einsum("rgd,cd->grc", query_head, key_head, preferred_element_type=jnp.float32)
            * scale
        )
        scores = jnp.where(allowed[None], scores, -1e30)
        row_max = jnp.max(scores, axis=-1, keepdims=True)
        exponent = jnp.exp(scores - row_max)
        denominator = jnp.sum(exponent, axis=-1)
        weights = exponent.astype(jnp.bfloat16)
        mixed_out = jnp.einsum("grc,cd->rgd", weights, val_head, preferred_element_type=jnp.float32)
        head_outputs.append(mixed_out / denominator.T[:, :, None])
    return jnp.stack(head_outputs, axis=1).reshape(rows_dev, QH * HD).astype(jnp.bfloat16)


def on_device(queries, keys, values, slot_order, doc_ids):
    slot_perm = slot_order[0, 0]
    outgoing = (
        jnp.take(queries, slot_perm, axis=0),
        jnp.take(keys, slot_perm, axis=0),
        jnp.take(values, slot_perm, axis=0),
    )
    group_q, group_k, group_v = (
        lax.all_to_all(outgoing[0], "grp", split_axis=0, concat_axis=0, tiled=True),
        lax.all_to_all(outgoing[1], "grp", split_axis=0, concat_axis=0, tiled=True),
        lax.all_to_all(outgoing[2], "grp", split_axis=0, concat_axis=0, tiled=True),
    )
    context = window_attention(group_q, group_k, group_v, doc_ids[0])
    returned = lax.all_to_all(context, "grp", split_axis=0, concat_axis=0, tiled=True)
    return jnp.zeros_like(returned).at[slot_perm].set(returned)


def solution(mesh):
    return jax.shard_map(
        on_device,
        mesh=mesh,
        in_specs=(
            P(("grp", "sp"), None),
            P(("grp", "sp"), None),
            P(("grp", "sp"), None),
            P("grp", "sp", None),
            P("grp", None),
        ),
        out_specs=P(("grp", "sp"), None),
        check_vma=False,
    )
```

profile of v0, /device:TPU:38, one launch (start us, length us, event | category | flops | bytes accessed | tf_op | source)
XLA Modules:
  0.0 221.1 jit_solution(835158785992941748)
XLA Ops:
  1.5 2.0 gather_fusion.1
  5.3 9.6 %all-to-all-start = ((bf16[16,8,1024]{2,1,0:T(8,128)(2,1)}), bf16[16,8,1024]{2,1,0:T(8,128)(2,1)S(1)}, u32[]{:S(2)}, u32[]{:S(2)}) async-start(bf16[16,8,1024]{2,1,0:T(8,128)(2,1)} %get-tuple-element.14), calls=%async_computation | async-start | bytes 524288 | tf_op jit(solution)/shard_map/all_to_all | solution.py:70
  17.5 7.4 %all-to-all-done = bf16[16,8,1024]{2,1,0:T(8,128)(2,1)S(1)} async-done(((bf16[16,8,1024]{2,1,0:T(8,128)(2,1)}), bf16[16,8,1024]{2,1,0:T(8,128)(2,1)S(1)}, u32[]{:S(2)}, u32[]{:S(2)}) %all-to-all-start) | async-done | bytes 262176 | tf_op jit(solution)/shard_map/all_to_all | solution.py:70
  24.9 4.6 %all-to-all-start.1 = ((bf16[16,8,1024]{2,1,0:T(8,128)(2,1)}), bf16[16,8,1024]{2,1,0:T(8,128)(2,1)S(1)}, u32[]{:S(2)}, u32[]{:S(2)}) async-start(bf16[16,8,1024]{2,1,0:T(8,128)(2,1)} %get-tuple-element.15), calls=%async_computation.1 | async-start | bytes 524288 | tf_op jit(solution)/shard_map/all_to_all | solution.py:69
  31.1 4.8 %collective-permute-start = (bf16[128,1024]{0,1:T(8,128)(2,1)S(1)}, bf16[128,1024]{0,1:T(8,128)(2,1)S(1)}, u32[]{:S(2)}, u32[]{:S(2)}) collective-permute-start(bf16[128,1024]{0,1:T(8,128)(2,1)S(1)} %copy.16), channel_id=1, source_target_pairs={{0,8},{1,9},{2,10},{3,11},{4,12},{5,13},{6,14},{7,15},{16,24},{17,... | collective-permute-start | bytes 786440 | tf_op jit(solution)/shard_map/ppermute | solution.py:14
  37.2 1.9 collective-permute-start.2
  39.4 7.3 %all-to-all-start.2 = ((bf16[16,8,5120]{2,1,0:T(8,128)(2,1)}), bf16[16,8,5120]{2,1,0:T(8,128)(2,1)}, u32[]{:S(2)}, u32[]{:S(2)}) async-start(bf16[16,8,5120]{2,1,0:T(8,128)(2,1)} %bitcast_select_fusion), calls=%async_computation.2 | async-start | bytes 2621440 | tf_op jit(solution)/shard_map/all_to_all | solution.py:68
  46.9 1.8 collective-permute-start.8
  50.0 4.3 %collective-permute-start.3 = (bf16[128,1024]{0,1:T(8,128)(2,1)S(1)}, bf16[128,1024]{0,1:T(8,128)(2,1)S(1)}, u32[]{:S(2)}, u32[]{:S(2)}) collective-permute-start(bf16[128,1024]{0,1:T(8,128)(2,1)S(1)} %copy.16), channel_id=1, source_target_pairs={{0,5},{1,6},{2,7},{3,8},{4,9},{5,10},{6,11},{7,12},{8,13},{9,14},{... | collective-permute-start | bytes 786440 | tf_op jit(solution)/shard_map/ppermute | solution.py:14
  54.4 19.8 %collective-permute-start.4 = (bf16[128,1024]{0,1:T(8,128)(2,1)S(1)}, bf16[128,1024]{0,1:T(8,128)(2,1)S(1)}, u32[]{:S(2)}, u32[]{:S(2)}) collective-permute-start(bf16[128,1024]{0,1:T(8,128)(2,1)S(1)} %copy.16), channel_id=1, source_target_pairs={{0,4},{1,5},{2,6},{3,7},{4,8},{5,9},{6,10},{7,11},{8,12},{9,13},{1... | collective-permute-start | bytes 786440 | tf_op jit(solution)/shard_map/ppermute | solution.py:14
  74.2 1.9 collective-permute-start.5
  76.3 4.3 %collective-permute-start.6 = (bf16[128,1024]{0,1:T(8,128)(2,1)S(1)}, bf16[128,1024]{0,1:T(8,128)(2,1)S(1)}, u32[]{:S(2)}, u32[]{:S(2)}) collective-permute-start(bf16[128,1024]{0,1:T(8,128)(2,1)S(1)} %copy.16), channel_id=1, source_target_pairs={{0,2},{1,3},{2,4},{3,5},{4,6},{5,7},{6,8},{7,9},{8,10},{9,11},{10,... | collective-permute-start | bytes 786440 | tf_op jit(solution)/shard_map/ppermute | solution.py:14
  80.6 1.9 collective-permute-start.7
  82.6 5.1 %collective-permute-done.5 = bf16[128,1024]{0,1:T(8,128)(2,1)S(1)} collective-permute-done((bf16[128,1024]{0,1:T(8,128)(2,1)S(1)}, bf16[128,1024]{0,1:T(8,128)(2,1)S(1)}, u32[]{:S(2)}, u32[]{:S(2)}) %collective-permute-start.5) | collective-permute-done | bytes 262176 | tf_op jit(solution)/shard_map/ppermute | solution.py:14
  87.7 1.9 collective-permute-start.10
  89.7 4.7 %collective-permute-done.6 = bf16[128,1024]{0,1:T(8,128)(2,1)S(1)} collective-permute-done((bf16[128,1024]{0,1:T(8,128)(2,1)S(1)}, bf16[128,1024]{0,1:T(8,128)(2,1)S(1)}, u32[]{:S(2)}, u32[]{:S(2)}) %collective-permute-start.6) | collective-permute-done | bytes 262176 | tf_op jit(solution)/shard_map/ppermute | solution.py:14
  94.4 1.9 collective-permute-start.11
  96.4 1.9 collective-permute-start.12
  98.5 23.6 %collective-permute-start.13 = (bf16[128,1024]{1,0:T(8,128)(2,1)S(1)}, bf16[128,1024]{1,0:T(8,128)(2,1)S(1)}, u32[]{:S(2)}, u32[]{:S(2)}) collective-permute-start(bf16[128,1024]{1,0:T(8,128)(2,1)S(1)} %bitcast.282), channel_id=1, source_target_pairs={{0,3},{1,4},{2,5},{3,6},{4,7},{5,8},{6,9},{7,10},{8,11},{9,12},{10... | collective-permute-start | bytes 786440 | tf_op jit(solution)/shard_map/ppermute | solution.py:14
  122.8 2.7 %collective-permute-start.14 = (bf16[128,1024]{1,0:T(8,128)(2,1)S(1)}, bf16[128,1024]{1,0:T(8,128)(2,1)S(1)}, u32[]{:S(2)}, u32[]{:S(2)}) collective-permute-start(bf16[128,1024]{1,0:T(8,128)(2,1)S(1)} %bitcast.283), channel_id=1, source_target_pairs={{0,2},{1,3},{2,4},{3,5},{4,6},{5,7},{6,8},{7,9},{8,10},{9,11},{10,... | collective-permute-start | bytes 786440 | tf_op jit(solution)/shard_map/ppermute | solution.py:14
  126.2 1.9 collective-permute-start.15
  131.4 4.9 %collective-permute-done.14 = bf16[128,1024]{1,0:T(8,128)(2,1)S(1)} collective-permute-done((bf16[128,1024]{1,0:T(8,128)(2,1)S(1)}, bf16[128,1024]{1,0:T(8,128)(2,1)S(1)}, u32[]{:S(2)}, u32[]{:S(2)}) %collective-permute-start.14) | collective-permute-done | bytes 262176 | tf_op jit(solution)/shard_map/ppermute | solution.py:14
  138.5 3.4 %reshape.128 = bf16[128,8,5,128]{3,2,1,0:T(8,128)(2,1)S(1)} reshape(bf16[16,8,5120]{2,1,0:T(8,128)(2,1)} %all-to-all-done.2) | data formatting | bytes 2621440 | tf_op jit(solution)/shard_map/reshape | solution.py:40
  142.3 1.6 fusion.182
  145.4 1.6 fusion.184
  147.0 1.6 fusion.185
  150.1 1.6 fusion.187
  153.3 1.6 fusion.189
  170.0 3.1 %copy.41 = bf16[128,8,5,128]{3,2,1,0:T(8,128)(2,1)S(1)} copy(bf16[128,8,5,128]{0,3,2,1:T(8,128)(2,1)} %fusion.133) | data formatting | bytes 2621440 | tf_op jit(solution)/shard_map/stack | solution.py:57
  173.1 2.3 %convert_element_type.37 = bf16[16,8,5120]{2,1,0:T(8,128)(2,1)} reshape(bf16[128,8,5,128]{3,2,1,0:T(8,128)(2,1)S(1)} %copy.41) | data formatting | bytes 2621440 | tf_op jit(solution)/shard_map/convert_element_type | solution.py:57
  175.4 42.1 %all_to_all.39 = bf16[16,8,5120]{2,1,0:T(8,128)(2,1)S(1)} all-to-all(bf16[16,8,5120]{2,1,0:T(8,128)(2,1)} %convert_element_type.37), channel_id=1, replica_groups=mesh['grp'=16,'sp'=16] {'grp'}, dimensions={0} | all-to-all | bytes 2621440 | tf_op jit(solution)/shard_map/all_to_all | solution.py:73
  217.5 3.6 %scatter_custom_fusion = bf16[128,5120]{1,0:T(8,128)(2,1)} fusion(s32[128]{0:T(128)} %copy-done.5, bf16[16,8,5120]{2,1,0:T(8,128)(2,1)S(1)} %all_to_all.39, bf16[]{:T(256)} %constant.11.clone.1), kind=kCustom, calls=%fused_computation.68 | custom fusion | bytes 2621952 | tf_op jit(solution)/shard_map/scatter | solution.py:74
  (86 shorter events, 38.1 us)
Async XLA Ops:
  0.0 16.2 %copy-start = (bf16[128,5120]{1,0:T(8,128)(2,1)S(1)}, bf16[128,5120]{1,0:T(8,128)(2,1)}, u32[]{:S(2)}) copy-start(bf16[128,5120]{1,0:T(8,128)(2,1)} %param.7) | copy-start | bytes 3932164
  0.0 3.5 %copy-start.1 = (bf16[128,1024]{1,0:T(8,128)(2,1)S(1)}, bf16[128,1024]{1,0:T(8,128)(2,1)}, u32[]{:S(2)}) copy-start(bf16[128,1024]{1,0:T(8,128)(2,1)} %param.8) | copy-start | bytes 786436
  3.5 11.9 %copy-start.6 = (s32[1,1,128]{2,1,0:T(1,128)S(1)}, s32[1,1,128]{2,1,0:T(1,128)}, u32[]{:S(2)}) copy-start(s32[1,1,128]{2,1,0:T(1,128)} %param.10) | copy-start | bytes 1540
  5.3 19.7 %all-to-all-start = ((bf16[16,8,1024]{2,1,0:T(8,128)(2,1)}), bf16[16,8,1024]{2,1,0:T(8,128)(2,1)S(1)}, u32[]{:S(2)}, u32[]{:S(2)}) async-start(bf16[16,8,1024]{2,1,0:T(8,128)(2,1)} %get-tuple-element.14), calls=%async_computation | async-start | bytes 524288 | tf_op jit(solution)/shard_map/all_to_all | solution.py:70
  16.2 1.3 copy-start.5
  17.5 13.2 %copy-start.2 = (s32[1,2048]{1,0:T(1,128)S(1)}, s32[1,2048]{1,0:T(1,128)}, u32[]{:S(2)}) copy-start(s32[1,2048]{1,0:T(1,128)} %param.11) | copy-start | bytes 24580
  24.9 14.5 %all-to-all-start.1 = ((bf16[16,8,1024]{2,1,0:T(8,128)(2,1)}), bf16[16,8,1024]{2,1,0:T(8,128)(2,1)S(1)}, u32[]{:S(2)}, u32[]{:S(2)}) async-start(bf16[16,8,1024]{2,1,0:T(8,128)(2,1)} %get-tuple-element.15), calls=%async_computation.1 | async-start | bytes 524288 | tf_op jit(solution)/shard_map/all_to_all | solution.py:69
  31.1 18.9 %collective-permute-start = (bf16[128,1024]{0,1:T(8,128)(2,1)S(1)}, bf16[128,1024]{0,1:T(8,128)(2,1)S(1)}, u32[]{:S(2)}, u32[]{:S(2)}) collective-permute-start(bf16[128,1024]{0,1:T(8,128)(2,1)S(1)} %copy.16), channel_id=1, source_target_pairs={{0,8},{1,9},{2,10},{3,11},{4,12},{5,13},{6,14},{7,15},{16,24},{17,... | collective-permute-start | bytes 786440 | tf_op jit(solution)/shard_map/ppermute | solution.py:14
  35.9 18.5 %collective-permute-start.1 = (bf16[128,1024]{0,1:T(8,128)(2,1)S(1)}, bf16[128,1024]{0,1:T(8,128)(2,1)S(1)}, u32[]{:S(2)}, u32[]{:S(2)}) collective-permute-start(bf16[128,1024]{0,1:T(8,128)(2,1)S(1)} %copy.16), channel_id=1, source_target_pairs={{0,7},{1,8},{2,9},{3,10},{4,11},{5,12},{6,13},{7,14},{8,15},{16,23... | collective-permute-start | bytes 786440 | tf_op jit(solution)/shard_map/ppermute | solution.py:14
  37.2 37.0 %collective-permute-start.2 = (bf16[128,1024]{0,1:T(8,128)(2,1)S(1)}, bf16[128,1024]{0,1:T(8,128)(2,1)S(1)}, u32[]{:S(2)}, u32[]{:S(2)}) collective-permute-start(bf16[128,1024]{0,1:T(8,128)(2,1)S(1)} %copy.16), channel_id=1, source_target_pairs={{0,6},{1,7},{2,8},{3,9},{4,10},{5,11},{6,12},{7,13},{8,14},{9,15},... | collective-permute-start | bytes 786440 | tf_op jit(solution)/shard_map/ppermute | solution.py:14
  39.4 99.1 %all-to-all-start.2 = ((bf16[16,8,5120]{2,1,0:T(8,128)(2,1)}), bf16[16,8,5120]{2,1,0:T(8,128)(2,1)}, u32[]{:S(2)}, u32[]{:S(2)}) async-start(bf16[16,8,5120]{2,1,0:T(8,128)(2,1)} %bitcast_select_fusion), calls=%async_computation.2 | async-start | bytes 2621440 | tf_op jit(solution)/shard_map/all_to_all | solution.py:68
  46.9 51.6 %collective-permute-start.8 = (bf16[128,1024]{1,0:T(8,128)(2,1)S(1)}, bf16[128,1024]{1,0:T(8,128)(2,1)S(1)}, u32[]{:S(2)}, u32[]{:S(2)}) collective-permute-start(bf16[128,1024]{1,0:T(8,128)(2,1)S(1)} %bitcast.277), channel_id=1, source_target_pairs={{0,8},{1,9},{2,10},{3,11},{4,12},{5,13},{6,14},{7,15},{16,24},{17,... | collective-permute-start | bytes 786440 | tf_op jit(solution)/shard_map/ppermute | solution.py:14
  48.7 74.2 %collective-permute-start.9 = (bf16[128,1024]{1,0:T(8,128)(2,1)S(1)}, bf16[128,1024]{1,0:T(8,128)(2,1)S(1)}, u32[]{:S(2)}, u32[]{:S(2)}) collective-permute-start(bf16[128,1024]{1,0:T(8,128)(2,1)S(1)} %bitcast.278), channel_id=1, source_target_pairs={{0,7},{1,8},{2,9},{3,10},{4,11},{5,12},{6,13},{7,14},{8,15},{16,23... | collective-permute-start | bytes 786440 | tf_op jit(solution)/shard_map/ppermute | solution.py:14
  50.0 26.3 %collective-permute-start.3 = (bf16[128,1024]{0,1:T(8,128)(2,1)S(1)}, bf16[128,1024]{0,1:T(8,128)(2,1)S(1)}, u32[]{:S(2)}, u32[]{:S(2)}) collective-permute-start(bf16[128,1024]{0,1:T(8,128)(2,1)S(1)} %copy.16), channel_id=1, source_target_pairs={{0,5},{1,6},{2,7},{3,8},{4,9},{5,10},{6,11},{7,12},{8,13},{9,14},{... | collective-permute-start | bytes 786440 | tf_op jit(solution)/shard_map/ppermute | solution.py:14
  54.4 26.3 %collective-permute-start.4 = (bf16[128,1024]{0,1:T(8,128)(2,1)S(1)}, bf16[128,1024]{0,1:T(8,128)(2,1)S(1)}, u32[]{:S(2)}, u32[]{:S(2)}) collective-permute-start(bf16[128,1024]{0,1:T(8,128)(2,1)S(1)} %copy.16), channel_id=1, source_target_pairs={{0,4},{1,5},{2,6},{3,7},{4,8},{5,9},{6,10},{7,11},{8,12},{9,13},{1... | collective-permute-start | bytes 786440 | tf_op jit(solution)/shard_map/ppermute | solution.py:14
  74.2 13.5 %collective-permute-start.5 = (bf16[128,1024]{0,1:T(8,128)(2,1)S(1)}, bf16[128,1024]{0,1:T(8,128)(2,1)S(1)}, u32[]{:S(2)}, u32[]{:S(2)}) collective-permute-start(bf16[128,1024]{0,1:T(8,128)(2,1)S(1)} %copy.16), channel_id=1, source_target_pairs={{0,3},{1,4},{2,5},{3,6},{4,7},{5,8},{6,9},{7,10},{8,11},{9,12},{10... | collective-permute-start | bytes 786440 | tf_op jit(solution)/shard_map/ppermute | solution.py:14
  76.3 18.1 %collective-permute-start.6 = (bf16[128,1024]{0,1:T(8,128)(2,1)S(1)}, bf16[128,1024]{0,1:T(8,128)(2,1)S(1)}, u32[]{:S(2)}, u32[]{:S(2)}) collective-permute-start(bf16[128,1024]{0,1:T(8,128)(2,1)S(1)} %copy.16), channel_id=1, source_target_pairs={{0,2},{1,3},{2,4},{3,5},{4,6},{5,7},{6,8},{7,9},{8,10},{9,11},{10,... | collective-permute-start | bytes 786440 | tf_op jit(solution)/shard_map/ppermute | solution.py:14
  80.6 15.7 %collective-permute-start.7 = (bf16[128,1024]{0,1:T(8,128)(2,1)S(1)}, bf16[128,1024]{0,1:T(8,128)(2,1)S(1)}, u32[]{:S(2)}, u32[]{:S(2)}) collective-permute-start(bf16[128,1024]{0,1:T(8,128)(2,1)S(1)} %copy.16), channel_id=1, source_target_pairs={{0,1},{1,2},{2,3},{3,4},{4,5},{5,6},{6,7},{7,8},{8,9},{9,10},{10,1... | collective-permute-start | bytes 786440 | tf_op jit(solution)/shard_map/ppermute | solution.py:14
  87.7 38.5 %collective-permute-start.10 = (bf16[128,1024]{1,0:T(8,128)(2,1)S(1)}, bf16[128,1024]{1,0:T(8,128)(2,1)S(1)}, u32[]{:S(2)}, u32[]{:S(2)}) collective-permute-start(bf16[128,1024]{1,0:T(8,128)(2,1)S(1)} %bitcast.279), channel_id=1, source_target_pairs={{0,6},{1,7},{2,8},{3,9},{4,10},{5,11},{6,12},{7,13},{8,14},{9,15},... | collective-permute-start | bytes 786440 | tf_op jit(solution)/shard_map/ppermute | solution.py:14
  94.4 34.5 %collective-permute-start.11 = (bf16[128,1024]{1,0:T(8,128)(2,1)S(1)}, bf16[128,1024]{1,0:T(8,128)(2,1)S(1)}, u32[]{:S(2)}, u32[]{:S(2)}) collective-permute-start(bf16[128,1024]{1,0:T(8,128)(2,1)S(1)} %bitcast.280), channel_id=1, source_target_pairs={{0,5},{1,6},{2,7},{3,8},{4,9},{5,10},{6,11},{7,12},{8,13},{9,14},{... | collective-permute-start | bytes 786440 | tf_op jit(solution)/shard_map/ppermute | solution.py:14
  96.4 33.2 %collective-permute-start.12 = (bf16[128,1024]{1,0:T(8,128)(2,1)S(1)}, bf16[128,1024]{1,0:T(8,128)(2,1)S(1)}, u32[]{:S(2)}, u32[]{:S(2)}) collective-permute-start(bf16[128,1024]{1,0:T(8,128)(2,1)S(1)} %bitcast.281), channel_id=1, source_target_pairs={{0,4},{1,5},{2,6},{3,7},{4,8},{5,9},{6,10},{7,11},{8,12},{9,13},{1... | collective-permute-start | bytes 786440 | tf_op jit(solution)/shard_map/ppermute | solution.py:14
  98.5 39.3 %copy-start.3 = (bf16[1152,1024]{0,1:T(8,128)(2,1)}, bf16[1152,1024]{0,1:T(8,128)(2,1)S(1)}, u32[]{:S(2)}) copy-start(bf16[1152,1024]{0,1:T(8,128)(2,1)S(1)} %constant_dynamic-update-slice_fusion) | copy-start | bytes 7077892
  98.5 32.2 %collective-permute-start.13 = (bf16[128,1024]{1,0:T(8,128)(2,1)S(1)}, bf16[128,1024]{1,0:T(8,128)(2,1)S(1)}, u32[]{:S(2)}, u32[]{:S(2)}) collective-permute-start(bf16[128,1024]{1,0:T(8,128)(2,1)S(1)} %bitcast.282), channel_id=1, source_target_pairs={{0,3},{1,4},{2,5},{3,6},{4,7},{5,8},{6,9},{7,10},{8,11},{9,12},{10... | collective-permute-start | bytes 786440 | tf_op jit(solution)/shard_map/ppermute | solution.py:14
  122.8 13.5 %collective-permute-start.14 = (bf16[128,1024]{1,0:T(8,128)(2,1)S(1)}, bf16[128,1024]{1,0:T(8,128)(2,1)S(1)}, u32[]{:S(2)}, u32[]{:S(2)}) collective-permute-start(bf16[128,1024]{1,0:T(8,128)(2,1)S(1)} %bitcast.283), channel_id=1, source_target_pairs={{0,2},{1,3},{2,4},{3,5},{4,6},{5,7},{6,8},{7,9},{8,10},{9,11},{10,... | collective-permute-start | bytes 786440 | tf_op jit(solution)/shard_map/ppermute | solution.py:14
  126.2 10.8 %collective-permute-start.15 = (bf16[128,1024]{1,0:T(8,128)(2,1)S(1)}, bf16[128,1024]{1,0:T(8,128)(2,1)S(1)}, u32[]{:S(2)}, u32[]{:S(2)}) collective-permute-start(bf16[128,1024]{1,0:T(8,128)(2,1)S(1)} %bitcast.284), channel_id=1, source_target_pairs={{0,1},{1,2},{2,3},{3,4},{4,5},{5,6},{6,7},{7,8},{8,9},{9,10},{10,1... | collective-permute-start | bytes 786440 | tf_op jit(solution)/shard_map/ppermute | solution.py:14
  154.8 1.7 copy-start.4
where the time goes:
time: 222 us; the launch traced here: 221 us
  starting transfers between devices  98.7 us (44%)
  blocking collectives  42.1 us (19%)
  local copies, waits for them, and re-layouts  26.2 us (12%)
  matrix products  23.1 us (10%)
  waiting for transfers between devices  22.7 us (10%)
  other arithmetic  7.73 us (3%)
    ppermute x16, starting transfers between devices, passed_along(): lax.ppermute(value, axis, [(source, source + steps) for source in range(f...  77.3 us
    all_to_all x1, blocking collectives, on_device(): lax.all_to_all(context, 'grp', split_axis=0, concat_axis=0, tiled=True)  42.1 us
    ppermute x16, waiting for transfers between devices, passed_along(): lax.ppermute(value, axis, [(source, source + steps) for source in range(f...  15.1 us
    dot_general x8, matrix products, window_attention(): jnp.einsum('rgd,cd->grc', query_head, key_head, preferred_element_type=jn...  12.5 us
    dot_general x8, matrix products, window_attention(): jnp.einsum('grc,cd->rgd', weights, val_head, preferred_element_type=jnp.f...  10.6 us
    all_to_all x1, starting transfers between devices, on_device(): lax.all_to_all(outgoing[2], 'grp', split_axis=0, concat_axis=0, tiled=True)  9.6 us
    unnamed x31, local copies, waits for them, and re-layouts  8.14 us
    all_to_all x1, waiting for transfers between devices, on_device(): lax.all_to_all(outgoing[2], 'grp', split_axis=0, concat_axis=0, tiled=True)  7.37 us
  transfers between devices with their start and end apart: 19, of which 6 were waited for; matrix products, arithmetic and copies ran while one was open for 5% of the time, Pallas kernels for 0%

commit v1 on v0

v1 whole, which is shorter than its diff:
```python
import functools

import jax
import jax.numpy as jnp
from jax import lax
from jax.experimental import pallas as pl
from jax.experimental.pallas import tpu as pltpu
from jax.sharding import Mesh
from jax.sharding import PartitionSpec as P

QH = 40
KVH = 8
HD = 128
GS = QH // KVH
NZ = 8
NSY = 32
NG = 4
ROWS = 8
CHUNKS = 2
GC = NG // CHUNKS
TILE_SY = 4
TROWS = TILE_SY * ROWS
NT = NSY // TILE_SY
SPAN_POS = TILE_SY * 64
MAXB = 5
NEG = -1e30
PLANE = ("yh", "x", "c", "yl")
VMEM_LIMIT = 48 * 1024 * 1024


def one_hot_t(slot):
    rows = lax.broadcasted_iota(jnp.int32, (128, 128), 0)
    return (rows == slot).astype(jnp.float32).astype(jnp.bfloat16)


def pick(onehot, x):
    return lax.dot_general(
        onehot, x, (((0,), (0,)), ((), ())), preferred_element_type=jnp.float32
    ).astype(jnp.bfloat16)


def kv_send_kernel(slot_ref, k_ref, v_ref, o_ref):
    onehot = one_hot_t(slot_ref[...])
    for part, ref in enumerate((k_ref, v_ref)):
        got = pick(onehot, ref[...])
        for h in range(KVH):
            for yl in range(2):
                for yh in range(2):
                    at = (yl * 2 + yh) * 32
                    o_ref[yh, h, yl, :, part * HD : (part + 1) * HD] = got[
                        at : at + 32, h * HD : (h + 1) * HD
                    ]


def q_send_kernel(slot_ref, q_ref, o_ref):
    onehot = one_hot_t(slot_ref[...])
    for h in range(KVH):
        got = pick(onehot, q_ref[:, h * GS * HD : (h + 1) * GS * HD])
        for yl in range(2):
            for yh in range(2):
                at = (yl * 2 + yh) * 32
                o_ref[yh, h, yl] = got[at : at + 32]


def put_back_kernel(slot_ref, *refs):
    parts, o_ref = refs[:-1], refs[-1]
    onehot = one_hot_t(slot_ref[...])
    for h in range(KVH):
        rows = [p[yh, h, yl] for yl in range(2) for yh in range(2) for p in parts]
        got = jnp.dot(onehot, jnp.concatenate(rows, axis=0), preferred_element_type=jnp.float32)
        o_ref[:, h * GS * HD : (h + 1) * GS * HD] = got.astype(jnp.bfloat16)


def attention_kernel(first_gg, info_ref, bounds_ref, q_ref, *refs):
    kv_refs, o_ref = refs[:NZ], refs[NZ]
    gg = pl.program_id(0) + first_gg
    row = info_ref[NZ + 1] + gg
    b1, b2, b3 = bounds_ref[row, 0], bounds_ref[row, 1], bounds_ref[row, 2]
    z0 = info_ref[NZ]

    q_iota = lax.broadcasted_iota(jnp.int32, (TROWS, 1), 0)
    q_rel = (q_iota // 8) * 64 + q_iota % 8 + z0 * 8
    k_iota = lax.broadcasted_iota(jnp.int32, (1, NZ * TROWS), 1)
    k_z = jnp.zeros_like(k_iota)
    for i in range(NZ):
        k_z = jnp.where(k_iota // TROWS == i, info_ref[i], k_z)
    k_in = k_iota % TROWS
    k_rel = (k_in // 8) * 64 + k_in % 8 + k_z * 8
    log2e_scale = (HD**-0.5) * 1.4426950408889634

    def tile(t, carry):
        first_pos = t * SPAN_POS + z0 * 8
        first_start = jnp.where(
            first_pos >= b3, b3, jnp.where(first_pos >= b2, b2, jnp.where(first_pos >= b1, b1, 0))
        )
        low = first_start // SPAN_POS
        q_pos = t * SPAN_POS + q_rel
        q_start = jnp.where(
            q_pos >= b3, b3, jnp.where(q_pos >= b2, b2, jnp.where(q_pos >= b1, b1, 0))
        )
        row0 = pl.multiple_of(t * TROWS, TROWS)
        q_tile = q_ref[0, :, pl.ds(row0, TROWS), :].reshape(GS * TROWS, HD)

        def work(count):
            keys, vals, oks = [], [], []
            for n in range(count):
                b = t - (count - 1) + n
                k0 = pl.multiple_of(b * TROWS, TROWS)
                for r in kv_refs:
                    keys.append(r[0, pl.ds(k0, TROWS), :HD])
                    vals.append(r[0, pl.ds(k0, TROWS), HD:])
                k_pos = b * SPAN_POS + k_rel
                oks.append((k_pos <= q_pos) & (k_pos >= q_start))
            keys = jnp.concatenate(keys, axis=0)
            vals = jnp.concatenate(vals, axis=0)
            ok = jnp.concatenate(oks, axis=1)
            s = lax.dot_general(
                q_tile, keys, (((1,), (1,)), ((), ())), preferred_element_type=jnp.float32
            )
            s = s.reshape(GS, TROWS, count * SPAN_POS)
            s = jnp.where(ok[None], s, NEG)
            m = jnp.max(s, axis=-1, keepdims=True)
            p = jnp.exp2((s - m) * log2e_scale)
            total = jnp.sum(p, axis=-1, keepdims=True)
            w = p.astype(jnp.bfloat16).reshape(GS * TROWS, count * SPAN_POS)
            out = jnp.dot(w, vals, preferred_element_type=jnp.float32)
            out = out.reshape(GS, TROWS, HD) / total
            for hh in range(GS):
                for i in range(TILE_SY):
                    o_ref[t * TILE_SY + i, 0, :, hh * HD : (hh + 1) * HD] = out[
                        hh, i * 8 : (i + 1) * 8
                    ].astype(jnp.bfloat16)

        for count in range(1, MAXB + 1):
            pl.when(t - low + 1 == count)(functools.partial(work, count))
        return carry

    lax.fori_loop(0, NT, tile, 0)


def attention(chunk, info, bounds, q, kvs):
    first = chunk * GC
    smem = pl.BlockSpec(memory_space=pltpu.SMEM)
    return pl.pallas_call(
        functools.partial(attention_kernel, first),
        grid=(GC,),
        out_shape=jax.ShapeDtypeStruct((NSY, GC, ROWS, GS * HD), jnp.bfloat16),
        in_specs=[smem, smem, pl.BlockSpec((1, GS, NSY * ROWS, HD), lambda g: (g + first, 0, 0, 0))]
        + [pl.BlockSpec((1, NSY * ROWS, 2 * HD), lambda g: (g, 0, 0))] * NZ,
        out_specs=pl.BlockSpec((NSY, 1, ROWS, GS * HD), lambda g: (0, g, 0, 0)),
        compiler_params=pltpu.CompilerParams(vmem_limit_bytes=VMEM_LIMIT),
        cost_estimate=pl.CostEstimate(
            flops=800_000_000, bytes_accessed=4_000_000, transcendentals=2_000_000
        ),
        name="attention",
    )(info, bounds, q, *kvs)


def whole(kernel, out_shape, *args):
    return pl.pallas_call(
        kernel,
        out_shape=out_shape,
        compiler_params=pltpu.CompilerParams(vmem_limit_bytes=VMEM_LIMIT),
        name=kernel.__name__,
    )(*args)


def swap(value, axes):
    return lax.all_to_all(value, axes, split_axis=0, concat_axis=0, tiled=True)


def along_z(value, step):
    return lax.ppermute(value, "z", [(i, (i + step) % NZ) for i in range(NZ)])


def on_device(queries, keys, values, slot_order, doc_ids):
    slot = slot_order[0]
    bf16 = jnp.bfloat16
    z0 = lax.axis_index("z")

    kv_out = whole(
        kv_send_kernel, jax.ShapeDtypeStruct((2, KVH, 2, 32, 2 * HD), bf16), slot, keys, values
    )
    kv = swap(kv_out.reshape(NSY, 32, 2 * HD), PLANE)
    kv = kv.reshape(NSY, NG, ROWS, 2 * HD).transpose(1, 0, 2, 3).reshape(NG, NSY * ROWS, 2 * HD)

    q_out = whole(q_send_kernel, jax.ShapeDtypeStruct((2, KVH, 2, 32, GS * HD), bf16), slot, queries)
    q = swap(q_out.reshape(NSY, 32, GS * HD), PLANE)
    q = q.reshape(NSY, NG, ROWS, GS, HD).transpose(1, 3, 0, 2, 4).reshape(NG, GS, NSY * ROWS, HD)

    edges = jnp.sum(doc_ids[0][None, :] < jnp.arange(1, 4, dtype=jnp.int32)[:, None], axis=1)
    edges = jnp.zeros((128,), jnp.int32).at[:3].set(edges.astype(jnp.int32))
    bounds = swap(jnp.broadcast_to(edges[None, None], (NZ, 8, 128)).reshape(NZ * 8, 128), ("z",))
    bounds = bounds.reshape(NZ, 8, 128)[:, 0]

    up = [kv[c * GC : (c + 1) * GC] for c in range(CHUNKS)]
    down = list(up)
    have = [[part] for part in up]
    for step in range(NZ // 2 - 1):
        for c in range(CHUNKS):
            up[c] = along_z(up[c], 1)
            down[c] = along_z(down[c], -1)
            have[c] += [up[c], down[c]]
    for c in range(CHUNKS):
        have[c].append(along_z(up[c], 1) if c % 2 == 0 else along_z(down[c], -1))
    offsets = [0, -1, 1, -2, 2, -3, 3, 4]
    info = jnp.stack([(z0 + o + NZ) % NZ for o in offsets] + [z0, lax.axis_index("yh") * NG])
    info = info.astype(jnp.int32)

    back = []
    for c in range(CHUNKS):
        out = attention(c, info, bounds, q, have[c])
        got = swap(out.reshape(NSY, GC * ROWS, GS * HD), PLANE)
        back.append(got.reshape(2, KVH, 2, GC * ROWS, GS * HD))
    return whole(
        put_back_kernel, jax.ShapeDtypeStruct((128, QH * HD), bf16), slot, *back
    )


def solution(mesh):
    fine = Mesh(mesh.devices.reshape(2, NZ, 2, 4, 2), ("yl", "z", "yh", "x", "c"))
    rows = P(("yl", "z", "yh", "x", "c"), None)
    return jax.shard_map(
        on_device,
        mesh=fine,
        in_specs=(rows, rows, rows, P(("yl", "z"), ("yh", "x", "c"), None), P(("yl", "z"), None)),
        out_specs=rows,
        check_vma=False,
    )
```

time: 222 us -> 149 us (0.67)
  the two profiles are of different devices: /device:TPU:38 before, /device:TPU:1 now
where the time goes in v1:
time: 149 us
  starting transfers between devices  51 us (34%)
  waiting for transfers between devices  45.1 us (30%)
  Pallas kernels  24.2 us (16%)
  blocking collectives  22.3 us (15%)
  local copies, waits for them, and re-layouts  5.01 us (3%)
    all_to_all x4, starting transfers between devices, swap(): return lax.all_to_all(value, axes, split_axis=0, concat_axis=0, tiled=True)  33.8 us
    ppermute x14, waiting for transfers between devices, along_z(): return lax.ppermute(value, 'z', [(i, (i + step) % NZ) for i in range(NZ)])  32.7 us
    all_to_all x1, blocking collectives, swap(): return lax.all_to_all(value, axes, split_axis=0, concat_axis=0, tiled=True)  22.3 us
    pallas_call x2, Pallas kernels, attention(): pl.pallas_call(functools.partial(attention_kernel, first), grid=(GC,), ou...  19.9 us
    ppermute x14, starting transfers between devices, along_z(): return lax.ppermute(value, 'z', [(i, (i + step) % NZ) for i in range(NZ)])  17.3 us
    all_to_all x4, waiting for transfers between devices, swap(): return lax.all_to_all(value, axes, split_axis=0, concat_axis=0, tiled=True)  12.4 us
    pallas_call x3, Pallas kernels, whole(): pl.pallas_call(kernel, out_shape=out_shape, compiler_params=pltpu.Compile...  4.29 us
  transfers between devices with their start and end apart: 18, of which 9 were waited for; matrix products, arithmetic and copies ran while one was open for 1% of the time, Pallas kernels for 15%

profile of v1, /device:TPU:1, one launch (start us, length us, event | category | flops | bytes accessed | tf_op | source)
XLA Modules:
  0.0 148.8 jit_solution(3185830090374160874)
XLA Ops:
  0.0 1.0 convert_reduce_fusion
  1.0 0.6 reshape.78
  1.6 9.0 %all-to-all-start = ((s32[8,8,128]{2,1,0:T(8,128)}), s32[8,8,128]{2,1,0:T(8,128)S(1)}, u32[]{:S(2)}, u32[]{:S(2)}) async-start(s32[8,8,128]{2,1,0:T(8,128)} %reshape.78), calls=%async_computation | async-start | bytes 65536 | tf_op jit(solution)/shard_map/all_to_all | solution.py:169
  10.7 0.9 copy-done.1
  11.6 0.9 copy-done.2
  12.6 0.7 copy-done.3
  13.2 1.1 kv_send_kernel.1
  14.3 3.2 %all-to-all-done = s32[8,8,128]{2,1,0:T(8,128)S(1)} async-done(((s32[8,8,128]{2,1,0:T(8,128)}), s32[8,8,128]{2,1,0:T(8,128)S(1)}, u32[]{:S(2)}, u32[]{:S(2)}) %all-to-all-start) | async-done | bytes 32800 | tf_op jit(solution)/shard_map/all_to_all | solution.py:169
  17.5 9.2 %all-to-all-start.2 = ((bf16[32,32,256]{2,1,0:T(8,128)(2,1)}), bf16[32,32,256]{2,1,0:T(8,128)(2,1)S(1)}, u32[]{:S(2)}, u32[]{:S(2)}) async-start(bf16[32,32,256]{2,1,0:T(8,128)(2,1)} %bitcast.17), calls=%async_computation.2 | async-start | bytes 1048576 | tf_op jit(solution)/shard_map/all_to_all | solution.py:169
  26.7 1.6 %q_send_kernel.1 = bf16[2,8,2,32,640]{4,3,2,1,0:T(8,128)(2,1)} custom-call(s32[1,128]{1,0:T(1,128)S(1)} %bitcast.49, bf16[128,5120]{1,0:T(8,128)(2,1)S(1)} %copy-done), custom_call_target="tpu_custom_call" | custom-call | tf_op jit(solution)/shard_map/q_send_kernel/pallas_call | solution.py:160
  28.3 9.2 %all-to-all-done.2 = bf16[32,32,256]{2,1,0:T(8,128)(2,1)S(1)} async-done(((bf16[32,32,256]{2,1,0:T(8,128)(2,1)}), bf16[32,32,256]{2,1,0:T(8,128)(2,1)S(1)}, u32[]{:S(2)}, u32[]{:S(2)}) %all-to-all-start.2) | async-done | bytes 524320 | tf_op jit(solution)/shard_map/all_to_all | solution.py:169
  37.6 6.0 %all-to-all-start.1 = ((bf16[32,32,640]{2,1,0:T(8,128)(2,1)}), bf16[32,32,640]{2,1,0:T(8,128)(2,1)}, u32[]{:S(2)}, u32[]{:S(2)}) async-start(bf16[32,32,640]{2,1,0:T(8,128)(2,1)} %bitcast.13), calls=%async_computation.1 | async-start | bytes 2621440 | tf_op jit(solution)/shard_map/all_to_all | solution.py:169
  43.6 0.4 collective-permute-start
  44.0 2.4 %collective-permute-start.1 = (bf16[2,256,256]{2,1,0:T(8,128)(2,1)S(1)}, bf16[2,256,256]{2,1,0:T(8,128)(2,1)S(1)}, u32[]{:S(2)}, u32[]{:S(2)}) collective-permute-start(bf16[2,256,256]{2,1,0:T(8,128)(2,1)S(1)} %bitcast.44), channel_id=1, source_target_pairs={{0,112},{16,0},{32,16},{48,32},{64,48},{80,64},{96,80},{112,96},{1... | collective-permute-start | bytes 786440 | tf_op jit(solution)/shard_map/ppermute | solution.py:173
  46.3 6.1 %collective-permute-done.refs_1_ = bf16[2,256,256]{2,1,0:T(8,128)(2,1)S(1)} collective-permute-done((bf16[2,256,256]{2,1,0:T(8,128)(2,1)S(1)}, bf16[2,256,256]{2,1,0:T(8,128)(2,1)S(1)}, u32[]{:S(2)}, u32[]{:S(2)}) %collective-permute-start) | collective-permute-done | bytes 262176 | tf_op jit(solution)/shard_map/ppermute | solution.py:173
  52.5 2.7 %collective-permute-start.8 = (bf16[2,256,256]{2,1,0:T(8,128)(2,1)S(1)}, bf16[2,256,256]{2,1,0:T(8,128)(2,1)S(1)}, u32[]{:S(2)}, u32[]{:S(2)}) collective-permute-start(bf16[2,256,256]{2,1,0:T(8,128)(2,1)S(1)} %bitcast.40), channel_id=1, source_target_pairs={{0,112},{16,0},{32,16},{48,32},{64,48},{80,64},{96,80},{112,96},{1... | collective-permute-start | bytes 786440 | tf_op jit(solution)/shard_map/ppermute | solution.py:173
  55.3 5.0 %collective-permute-done.2.refs_3_ = bf16[2,256,256]{2,1,0:T(8,128)(2,1)S(1)} collective-permute-done((bf16[2,256,256]{2,1,0:T(8,128)(2,1)S(1)}, bf16[2,256,256]{2,1,0:T(8,128)(2,1)S(1)}, u32[]{:S(2)}, u32[]{:S(2)}) %collective-permute-start.2) | collective-permute-done | bytes 262176 | tf_op jit(solution)/shard_map/ppermute | solution.py:173
  60.5 2.7 %collective-permute-start.10 = (bf16[2,256,256]{2,1,0:T(8,128)(2,1)S(1)}, bf16[2,256,256]{2,1,0:T(8,128)(2,1)}, u32[]{:S(2)}, u32[]{:S(2)}) collective-permute-start(bf16[2,256,256]{2,1,0:T(8,128)(2,1)S(1)} %collective-permute-done.8.refs_2_), channel_id=1, source_target_pairs={{0,112},{16,0},{32,16},{48,32},{64,48},{80,64},{96,80},{112,96},{1... | collective-permute-start | bytes 786440 | tf_op jit(solution)/shard_map/ppermute | solution.py:173
  63.3 1.8 %collective-permute-done.3.refs_4_ = bf16[2,256,256]{2,1,0:T(8,128)(2,1)S(1)} collective-permute-done((bf16[2,256,256]{2,1,0:T(8,128)(2,1)S(1)}, bf16[2,256,256]{2,1,0:T(8,128)(2,1)S(1)}, u32[]{:S(2)}, u32[]{:S(2)}) %collective-permute-start.3) | collective-permute-done | bytes 262176 | tf_op jit(solution)/shard_map/ppermute | solution.py:173
  65.0 3.4 %collective-permute-start.5 = (bf16[2,256,256]{2,1,0:T(8,128)(2,1)S(1)}, bf16[2,256,256]{2,1,0:T(8,128)(2,1)}, u32[]{:S(2)}, u32[]{:S(2)}) collective-permute-start(bf16[2,256,256]{2,1,0:T(8,128)(2,1)S(1)} %collective-permute-done.3.refs_4_), channel_id=1, source_target_pairs={{0,112},{16,0},{32,16},{48,32},{64,48},{80,64},{96,80},{112,96},{1... | collective-permute-start | bytes 786440 | tf_op jit(solution)/shard_map/ppermute | solution.py:173
  68.5 1.7 %copy_bitcast_fusion.q_ref = bf16[4,5,256,128]{3,2,1,0:T(8,128)(2,1)S(1)} fusion(bf16[32,32,640]{2,1,0:T(8,128)(2,1)} %all-to-all-done.1), kind=kLoop, calls=%fused_computation | loop fusion | bytes 2621440 | tf_op jit(solution)/shard_map/reshape | solution.py:189
  70.1 6.1 %collective-permute-done.5.refs_6_ = bf16[2,256,256]{2,1,0:T(8,128)(2,1)} collective-permute-done((bf16[2,256,256]{2,1,0:T(8,128)(2,1)S(1)}, bf16[2,256,256]{2,1,0:T(8,128)(2,1)}, u32[]{:S(2)}, u32[]{:S(2)}) %collective-permute-start.5) | collective-permute-done | bytes 262176 | tf_op jit(solution)/shard_map/ppermute | solution.py:173
  76.3 2.4 %collective-permute-done.6.refs_7_ = bf16[2,256,256]{2,1,0:T(8,128)(2,1)} collective-permute-done((bf16[2,256,256]{2,1,0:T(8,128)(2,1)S(1)}, bf16[2,256,256]{2,1,0:T(8,128)(2,1)}, u32[]{:S(2)}, u32[]{:S(2)}) %collective-permute-start.6) | collective-permute-done | bytes 262176 | tf_op jit(solution)/shard_map/ppermute | solution.py:173
  78.6 10.5 %attention.2 = bf16[32,2,8,640]{3,2,1,0:T(8,128)(2,1)} custom-call(s32[10]{0:T(128)S(1)} %stack.43.info_ref, s32[8,128]{1,0:T(8,128)S(1)} %bitcast.46, bf16[4,5,256,128]{3,2,1,0:T(8,128)(2,1)S(1)} %copy_bitcast_fusion.q_ref, bf16[2,256,256]{2,1,0:T(8,128)(2,1)S(1)} %bitcast.45, bf16[2,256,256]{2,1,0:T(8,128)(2,1)S(1)} %collective-permute-done.refs_1_, ...), custom_call_target="tpu_custom_call" | custom-call | flops 800000000 | bytes 4000000 | tf_op jit(solution)/shard_map/attention/pallas_call | solution.py:144
  89.1 9.6 %all-to-all-start.3 = ((bf16[32,16,640]{2,1,0:T(8,128)(2,1)}), bf16[32,16,640]{2,1,0:T(8,128)(2,1)S(1)}, u32[]{:S(2)}, u32[]{:S(2)}) async-start(bf16[32,16,640]{2,1,0:T(8,128)(2,1)} %bitcast.21), calls=%async_computation.3 | async-start | bytes 1310720 | tf_op jit(solution)/shard_map/all_to_all | solution.py:169
  98.9 2.7 %collective-permute-start.12 = (bf16[2,256,256]{2,1,0:T(8,128)(2,1)}, bf16[2,256,256]{2,1,0:T(8,128)(2,1)S(1)}, u32[]{:S(2)}, u32[]{:S(2)}) collective-permute-start(bf16[2,256,256]{2,1,0:T(8,128)(2,1)} %collective-permute-done.10.refs_4_), channel_id=1, source_target_pairs={{0,112},{16,0},{32,16},{48,32},{64,48},{80,64},{96,80},{112,96},{1... | collective-permute-start | bytes 786440 | tf_op jit(solution)/shard_map/ppermute | solution.py:173
  101.5 6.2 %collective-permute-done.9.refs_3_ = bf16[2,256,256]{2,1,0:T(8,128)(2,1)S(1)} collective-permute-done((bf16[2,256,256]{2,1,0:T(8,128)(2,1)}, bf16[2,256,256]{2,1,0:T(8,128)(2,1)S(1)}, u32[]{:S(2)}, u32[]{:S(2)}) %collective-permute-start.9) | collective-permute-done | bytes 262176 | tf_op jit(solution)/shard_map/ppermute | solution.py:173
  107.7 2.7 %collective-permute-start.13 = (bf16[2,256,256]{2,1,0:T(8,128)(2,1)S(1)}, bf16[2,256,256]{2,1,0:T(8,128)(2,1)S(1)}, u32[]{:S(2)}, u32[]{:S(2)}) collective-permute-start(bf16[2,256,256]{2,1,0:T(8,128)(2,1)S(1)} %collective-permute-done.12.refs_6_), channel_id=1, source_target_pairs={{0,112},{16,0},{32,16},{48,32},{64,48},{80,64},{96,80},{112,96},{1... | collective-permute-start | bytes 786440 | tf_op jit(solution)/shard_map/ppermute | solution.py:173
  110.4 5.1 %collective-permute-done.11.refs_5_ = bf16[2,256,256]{2,1,0:T(8,128)(2,1)S(1)} collective-permute-done((bf16[2,256,256]{2,1,0:T(8,128)(2,1)S(1)}, bf16[2,256,256]{2,1,0:T(8,128)(2,1)S(1)}, u32[]{:S(2)}, u32[]{:S(2)}) %collective-permute-start.11) | collective-permute-done | bytes 262176 | tf_op jit(solution)/shard_map/ppermute | solution.py:173
  115.5 9.4 %attention.3 = bf16[32,2,8,640]{3,2,1,0:T(8,128)(2,1)S(1)} custom-call(s32[10]{0:T(128)S(1)} %stack.43.info_ref, s32[8,128]{1,0:T(8,128)S(1)} %bitcast.47, bf16[4,5,256,128]{3,2,1,0:T(8,128)(2,1)S(1)} %copy_bitcast_fusion.q_ref, bf16[2,256,256]{2,1,0:T(8,128)(2,1)S(1)} %bitcast.42, bf16[2,256,256]{2,1,0:T(8,128)(2,1)} %collective-permute-done.7.refs_1_, ...), custom_call_target="tpu_custom_call" | custom-call | flops 800000000 | bytes 4000000 | tf_op jit(solution)/shard_map/attention/pallas_call | solution.py:144
  124.9 22.3 %all_to_all.26 = bf16[32,16,640]{2,1,0:T(8,128)(2,1)S(1)} all-to-all(bf16[32,16,640]{2,1,0:T(8,128)(2,1)S(1)} %bitcast.37), channel_id=1, replica_groups=mesh['yl'=2,'z'=8,'yh'=2,'x'=4,'c'=2] {'yh','x','c','yl'}, dimensions={0} | all-to-all | bytes 1310720 | tf_op jit(solution)/shard_map/all_to_all | solution.py:169
  147.2 1.6 %put_back_kernel.1 = bf16[128,5120]{1,0:T(8,128)(2,1)} custom-call(s32[1,128]{1,0:T(1,128)S(1)} %bitcast.50, bf16[2,8,2,16,640]{4,3,2,1,0:T(8,128)(2,1)S(1)} %bitcast.38, bf16[2,8,2,16,640]{4,3,2,1,0:T(8,128)(2,1)S(1)} %bitcast.39), custom_call_target="tpu_custom_call" | custom-call | tf_op jit(solution)/shard_map/put_back_kernel/pallas_call | solution.py:160
  (30 shorter events, 0.5 us)
Async XLA Ops:
  0.0 26.7 %copy-start = (bf16[128,5120]{1,0:T(8,128)(2,1)S(1)}, bf16[128,5120]{1,0:T(8,128)(2,1)}, u32[]{:S(2)}) copy-start(bf16[128,5120]{1,0:T(8,128)(2,1)} %q_ref.1) | copy-start | bytes 3932164
  1.6 15.9 %all-to-all-start = ((s32[8,8,128]{2,1,0:T(8,128)}), s32[8,8,128]{2,1,0:T(8,128)S(1)}, u32[]{:S(2)}, u32[]{:S(2)}) async-start(s32[8,8,128]{2,1,0:T(8,128)} %reshape.78), calls=%async_computation | async-start | bytes 65536 | tf_op jit(solution)/shard_map/all_to_all | solution.py:169
  10.6 0.9 copy-start.1
  11.6 0.9 copy-start.2
  12.5 0.7 copy-start.3
  13.2 13.5 %copy-start.4 = (s32[1,1,128]{2,1,0:T(1,128)S(1)}, s32[1,1,128]{2,1,0:T(1,128)}, u32[]{:S(2)}) copy-start(s32[1,1,128]{2,1,0:T(1,128)} %param.10) | copy-start | bytes 1540
  17.5 20.0 %all-to-all-start.2 = ((bf16[32,32,256]{2,1,0:T(8,128)(2,1)}), bf16[32,32,256]{2,1,0:T(8,128)(2,1)S(1)}, u32[]{:S(2)}, u32[]{:S(2)}) async-start(bf16[32,32,256]{2,1,0:T(8,128)(2,1)} %bitcast.17), calls=%async_computation.2 | async-start | bytes 1048576 | tf_op jit(solution)/shard_map/all_to_all | solution.py:169
  37.6 30.9 %all-to-all-start.1 = ((bf16[32,32,640]{2,1,0:T(8,128)(2,1)}), bf16[32,32,640]{2,1,0:T(8,128)(2,1)}, u32[]{:S(2)}, u32[]{:S(2)}) async-start(bf16[32,32,640]{2,1,0:T(8,128)(2,1)} %bitcast.13), calls=%async_computation.1 | async-start | bytes 2621440 | tf_op jit(solution)/shard_map/all_to_all | solution.py:169
  43.6 8.9 %collective-permute-start = (bf16[2,256,256]{2,1,0:T(8,128)(2,1)S(1)}, bf16[2,256,256]{2,1,0:T(8,128)(2,1)S(1)}, u32[]{:S(2)}, u32[]{:S(2)}) collective-permute-start(bf16[2,256,256]{2,1,0:T(8,128)(2,1)S(1)} %bitcast.43), channel_id=1, source_target_pairs={{0,16},{16,32},{32,48},{48,64},{64,80},{80,96},{96,112},{112,0},{1... | collective-permute-start | bytes 786440 | tf_op jit(solution)/shard_map/ppermute | solution.py:173
  44.0 11.3 %collective-permute-start.1 = (bf16[2,256,256]{2,1,0:T(8,128)(2,1)S(1)}, bf16[2,256,256]{2,1,0:T(8,128)(2,1)S(1)}, u32[]{:S(2)}, u32[]{:S(2)}) collective-permute-start(bf16[2,256,256]{2,1,0:T(8,128)(2,1)S(1)} %bitcast.44), channel_id=1, source_target_pairs={{0,112},{16,0},{32,16},{48,32},{64,48},{80,64},{96,80},{112,96},{1... | collective-permute-start | bytes 786440 | tf_op jit(solution)/shard_map/ppermute | solution.py:173
  52.5 7.9 %collective-permute-start.2 = (bf16[2,256,256]{2,1,0:T(8,128)(2,1)S(1)}, bf16[2,256,256]{2,1,0:T(8,128)(2,1)S(1)}, u32[]{:S(2)}, u32[]{:S(2)}) collective-permute-start(bf16[2,256,256]{2,1,0:T(8,128)(2,1)S(1)} %collective-permute-done.refs_1_), channel_id=1, source_target_pairs={{0,16},{16,32},{32,48},{48,64},{64,80},{80,96},{96,112},{112,0},{1... | collective-permute-start | bytes 786440 | tf_op jit(solution)/shard_map/ppermute | solution.py:173
  52.5 8.0 %collective-permute-start.8 = (bf16[2,256,256]{2,1,0:T(8,128)(2,1)S(1)}, bf16[2,256,256]{2,1,0:T(8,128)(2,1)S(1)}, u32[]{:S(2)}, u32[]{:S(2)}) collective-permute-start(bf16[2,256,256]{2,1,0:T(8,128)(2,1)S(1)} %bitcast.40), channel_id=1, source_target_pairs={{0,112},{16,0},{32,16},{48,32},{64,48},{80,64},{96,80},{112,96},{1... | collective-permute-start | bytes 786440 | tf_op jit(solution)/shard_map/ppermute | solution.py:173
  55.2 9.8 %collective-permute-start.3 = (bf16[2,256,256]{2,1,0:T(8,128)(2,1)S(1)}, bf16[2,256,256]{2,1,0:T(8,128)(2,1)S(1)}, u32[]{:S(2)}, u32[]{:S(2)}) collective-permute-start(bf16[2,256,256]{2,1,0:T(8,128)(2,1)S(1)} %collective-permute-done.1.refs_2_), channel_id=1, source_target_pairs={{0,112},{16,0},{32,16},{48,32},{64,48},{80,64},{96,80},{112,96},{1... | collective-permute-start | bytes 786440 | tf_op jit(solution)/shard_map/ppermute | solution.py:173
  60.3 8.1 %collective-permute-start.4 = (bf16[2,256,256]{2,1,0:T(8,128)(2,1)S(1)}, bf16[2,256,256]{2,1,0:T(8,128)(2,1)S(1)}, u32[]{:S(2)}, u32[]{:S(2)}) collective-permute-start(bf16[2,256,256]{2,1,0:T(8,128)(2,1)S(1)} %collective-permute-done.2.refs_3_), channel_id=1, source_target_pairs={{0,16},{16,32},{32,48},{48,64},{64,80},{80,96},{96,112},{112,0},{1... | collective-permute-start | bytes 786440 | tf_op jit(solution)/shard_map/ppermute | solution.py:173
  60.4 38.3 %collective-permute-start.7 = (bf16[2,256,256]{2,1,0:T(8,128)(2,1)S(1)}, bf16[2,256,256]{2,1,0:T(8,128)(2,1)}, u32[]{:S(2)}, u32[]{:S(2)}) collective-permute-start(bf16[2,256,256]{2,1,0:T(8,128)(2,1)S(1)} %bitcast.41), channel_id=1, source_target_pairs={{0,16},{16,32},{32,48},{48,64},{64,80},{80,96},{96,112},{112,0},{1... | collective-permute-start | bytes 786440 | tf_op jit(solution)/shard_map/ppermute | solution.py:173
  60.5 38.3 %collective-permute-start.10 = (bf16[2,256,256]{2,1,0:T(8,128)(2,1)S(1)}, bf16[2,256,256]{2,1,0:T(8,128)(2,1)}, u32[]{:S(2)}, u32[]{:S(2)}) collective-permute-start(bf16[2,256,256]{2,1,0:T(8,128)(2,1)S(1)} %collective-permute-done.8.refs_2_), channel_id=1, source_target_pairs={{0,112},{16,0},{32,16},{48,32},{64,48},{80,64},{96,80},{112,96},{1... | collective-permute-start | bytes 786440 | tf_op jit(solution)/shard_map/ppermute | solution.py:173
  65.0 11.2 %collective-permute-start.5 = (bf16[2,256,256]{2,1,0:T(8,128)(2,1)S(1)}, bf16[2,256,256]{2,1,0:T(8,128)(2,1)}, u32[]{:S(2)}, u32[]{:S(2)}) collective-permute-start(bf16[2,256,256]{2,1,0:T(8,128)(2,1)S(1)} %collective-permute-done.3.refs_4_), channel_id=1, source_target_pairs={{0,112},{16,0},{32,16},{48,32},{64,48},{80,64},{96,80},{112,96},{1... | collective-permute-start | bytes 786440 | tf_op jit(solution)/shard_map/ppermute | solution.py:173
  68.4 10.2 %collective-permute-start.6 = (bf16[2,256,256]{2,1,0:T(8,128)(2,1)S(1)}, bf16[2,256,256]{2,1,0:T(8,128)(2,1)}, u32[]{:S(2)}, u32[]{:S(2)}) collective-permute-start(bf16[2,256,256]{2,1,0:T(8,128)(2,1)S(1)} %collective-permute-done.4.refs_5_), channel_id=1, source_target_pairs={{0,16},{16,32},{32,48},{48,64},{64,80},{80,96},{96,112},{112,0},{1... | collective-permute-start | bytes 786440 | tf_op jit(solution)/shard_map/ppermute | solution.py:173
  89.1 35.8 %all-to-all-start.3 = ((bf16[32,16,640]{2,1,0:T(8,128)(2,1)}), bf16[32,16,640]{2,1,0:T(8,128)(2,1)S(1)}, u32[]{:S(2)}, u32[]{:S(2)}) async-start(bf16[32,16,640]{2,1,0:T(8,128)(2,1)} %bitcast.21), calls=%async_computation.3 | async-start | bytes 1310720 | tf_op jit(solution)/shard_map/all_to_all | solution.py:169
  98.8 9.0 %collective-permute-start.9 = (bf16[2,256,256]{2,1,0:T(8,128)(2,1)}, bf16[2,256,256]{2,1,0:T(8,128)(2,1)S(1)}, u32[]{:S(2)}, u32[]{:S(2)}) collective-permute-start(bf16[2,256,256]{2,1,0:T(8,128)(2,1)} %collective-permute-done.7.refs_1_), channel_id=1, source_target_pairs={{0,16},{16,32},{32,48},{48,64},{64,80},{80,96},{96,112},{112,0},{1... | collective-permute-start | bytes 786440 | tf_op jit(solution)/shard_map/ppermute | solution.py:173
  98.9 8.9 %collective-permute-start.12 = (bf16[2,256,256]{2,1,0:T(8,128)(2,1)}, bf16[2,256,256]{2,1,0:T(8,128)(2,1)S(1)}, u32[]{:S(2)}, u32[]{:S(2)}) collective-permute-start(bf16[2,256,256]{2,1,0:T(8,128)(2,1)} %collective-permute-done.10.refs_4_), channel_id=1, source_target_pairs={{0,112},{16,0},{32,16},{48,32},{64,48},{80,64},{96,80},{112,96},{1... | collective-permute-start | bytes 786440 | tf_op jit(solution)/shard_map/ppermute | solution.py:173
  107.7 7.8 %collective-permute-start.11 = (bf16[2,256,256]{2,1,0:T(8,128)(2,1)S(1)}, bf16[2,256,256]{2,1,0:T(8,128)(2,1)S(1)}, u32[]{:S(2)}, u32[]{:S(2)}) collective-permute-start(bf16[2,256,256]{2,1,0:T(8,128)(2,1)S(1)} %collective-permute-done.9.refs_3_), channel_id=1, source_target_pairs={{0,16},{16,32},{32,48},{48,64},{64,80},{80,96},{96,112},{112,0},{1... | collective-permute-start | bytes 786440 | tf_op jit(solution)/shard_map/ppermute | solution.py:173
  107.7 7.8 %collective-permute-start.13 = (bf16[2,256,256]{2,1,0:T(8,128)(2,1)S(1)}, bf16[2,256,256]{2,1,0:T(8,128)(2,1)S(1)}, u32[]{:S(2)}, u32[]{:S(2)}) collective-permute-start(bf16[2,256,256]{2,1,0:T(8,128)(2,1)S(1)} %collective-permute-done.12.refs_6_), channel_id=1, source_target_pairs={{0,112},{16,0},{32,16},{48,32},{64,48},{80,64},{96,80},{112,96},{1... | collective-permute-start | bytes 786440 | tf_op jit(solution)/shard_map/ppermute | solution.py:173

commit v2 on v1

v2 whole, which is shorter than its diff:
```python
import functools

import jax
import jax.numpy as jnp
from jax import lax
from jax.experimental import pallas as pl
from jax.experimental.pallas import tpu as pltpu
from jax.sharding import Mesh
from jax.sharding import PartitionSpec as P

QH = 40
KVH = 8
HD = 128
GS = QH // KVH
NZ = 8
NSY = 32
NG = 4
ROWS = 8
KROWS = NSY * ROWS
CHUNKS = 2
GC = NG // CHUNKS
TILE_SY = 8
TROWS = TILE_SY * ROWS
NT = NSY // TILE_SY
TILE_POS = TILE_SY * 64
BLOCK_POS = 256
BLOCK_ROWS = BLOCK_POS // NZ
TILE_BLOCKS = TILE_POS // BLOCK_POS
MAXB = TILE_BLOCKS + 4
NEG = -1e30
PLANE = ("yh", "x", "c", "yl")


def one_hot_t(slot):
    rows = lax.broadcasted_iota(jnp.int32, (128, 128), 0)
    return (rows == slot).astype(jnp.float32).astype(jnp.bfloat16)


def pick(onehot, x):
    return lax.dot_general(
        onehot, x, (((0,), (0,)), ((), ())), preferred_element_type=jnp.float32
    ).astype(jnp.bfloat16)


def kv_send_kernel(slot_ref, k_ref, v_ref, o_ref):
    onehot = one_hot_t(slot_ref[...])
    for part, ref in enumerate((k_ref, v_ref)):
        got = pick(onehot, ref[...])
        for h in range(KVH):
            for yl in range(2):
                for yh in range(2):
                    at = (yl * 2 + yh) * 32
                    o_ref[yh, h, yl, :, part * HD : (part + 1) * HD] = got[
                        at : at + 32, h * HD : (h + 1) * HD
                    ]


def ring_kernel(kv_ref, doc_ref, *o_refs):
    doc = doc_ref[...]
    lane = lax.broadcasted_iota(jnp.int32, (16, 2 * HD), 1)
    extra = jnp.zeros((16, 2 * HD), jnp.float32)
    for i in range(3):
        edge = jnp.sum((doc <= i).astype(jnp.int32), axis=1, keepdims=True)
        extra = jnp.where(lane == 2 * i, (edge // 64).astype(jnp.float32), extra)
        extra = jnp.where(lane == 2 * i + 1, (edge % 64).astype(jnp.float32), extra)
    rows = [kv_ref[sy].astype(jnp.float32) for sy in range(NSY)]
    for c, o_ref in enumerate(o_refs):
        for g in range(GC):
            at = (c * GC + g) * ROWS
            part = jnp.concatenate([r[at : at + ROWS] for r in rows], axis=0)
            o_ref[g * KROWS : (g + 1) * KROWS, :] = part.astype(jnp.bfloat16)
        o_ref[GC * KROWS :, :] = extra.astype(jnp.bfloat16)


def q_send_kernel(slot_ref, q_ref, o_ref):
    onehot = one_hot_t(slot_ref[...])
    for h in range(KVH):
        got = pick(onehot, q_ref[:, h * GS * HD : (h + 1) * GS * HD])
        for yl in range(2):
            for yh in range(2):
                at = (yl * 2 + yh) * 32
                o_ref[yh, h, yl] = got[at : at + 32]


def put_back_kernel(slot_ref, *refs):
    parts, o_ref = refs[:-1], refs[-1]
    onehot = one_hot_t(slot_ref[...])
    for h in range(KVH):
        rows = [p[yh, h, yl] for yl in range(2) for yh in range(2) for p in parts]
        got = jnp.dot(onehot, jnp.concatenate(rows, axis=0), preferred_element_type=jnp.float32)
        o_ref[:, h * GS * HD : (h + 1) * GS * HD] = got.astype(jnp.bfloat16)


def doc_start(pos, inner):
    b1, b2, b3 = inner
    return jnp.where(pos >= b3, b3, jnp.where(pos >= b2, b2, jnp.where(pos >= b1, b1, 0)))


def attention_kernel(info_ref, q_ref, *refs):
    kv_refs, o_ref = [refs[c * NZ : (c + 1) * NZ] for c in range(CHUNKS)], refs[-1]
    z0 = info_ref[NZ]
    q_iota = lax.broadcasted_iota(jnp.int32, (TROWS, 1), 0)
    q_rel = (q_iota // 8) * 64 + q_iota % 8 + z0 * 8
    k_iota = lax.broadcasted_iota(jnp.int32, (1, BLOCK_POS), 1)
    k_z = jnp.zeros_like(k_iota)
    for i in range(NZ):
        k_z = jnp.where(k_iota // BLOCK_ROWS == i, info_ref[i], k_z)
    k_in = k_iota % BLOCK_ROWS
    k_rel = (k_in // 8) * 64 + k_in % 8 + k_z * 8
    scale = (HD**-0.5) * 1.4426950408889634
    extras = [r[GC * KROWS :, :HD].astype(jnp.float32) for r in kv_refs[0]]
    inner = []
    for gg in range(NG):
        mine = jnp.zeros_like(extras[0])
        for i in range(NZ):
            mine = jnp.where(info_ref[i] == info_ref[NZ + 1] + gg, extras[i], mine)
        found = [mine[0, lane].astype(jnp.int32) for lane in range(6)]
        inner.append([found[2 * i] * 64 + found[2 * i + 1] for i in range(3)])

    def tile(t, carry):
        first_pos = t * TILE_POS + z0 * 8
        low = doc_start(first_pos, inner[0])
        for g in range(1, NG):
            low = jnp.minimum(low, doc_start(first_pos, inner[g]))
        low = low // BLOCK_POS
        top = (t + 1) * TILE_BLOCKS - 1
        q_pos = t * TILE_POS + q_rel
        row0 = pl.multiple_of(t * TROWS, TROWS)

        def work(count):
            for g in range(NG):
                q_start = doc_start(q_pos, inner[g])
                q_tile = q_ref[g, :, pl.ds(row0, TROWS), :].reshape(GS * TROWS, HD)
                keys, vals, oks = [], [], []
                for n in range(count):
                    block = top - (count - 1) + n
                    k0 = pl.multiple_of(g % GC * KROWS + block * BLOCK_ROWS, BLOCK_ROWS)
                    for r in kv_refs[g // GC]:
                        keys.append(r[pl.ds(k0, BLOCK_ROWS), :HD])
                        vals.append(r[pl.ds(k0, BLOCK_ROWS), HD:])
                    k_pos = block * BLOCK_POS + k_rel
                    oks.append((k_pos <= q_pos) & (k_pos >= q_start))
                keys = jnp.concatenate(keys, axis=0)
                vals = jnp.concatenate(vals, axis=0)
                vals = jnp.concatenate([vals, jnp.ones_like(vals)], axis=1)
                ok = jnp.concatenate(oks, axis=1)
                s = lax.dot_general(
                    q_tile, keys, (((1,), (1,)), ((), ())), preferred_element_type=jnp.float32
                )
                s = s.reshape(GS, TROWS, count * BLOCK_POS)
                s = jnp.where(ok[None], s, NEG)
                m = jnp.max(s, axis=-1, keepdims=True)
                p = jnp.exp2((s - m) * scale)
                w = p.astype(jnp.bfloat16).reshape(GS * TROWS, count * BLOCK_POS)
                out = jnp.dot(w, vals, preferred_element_type=jnp.float32)
                out = (out[:, :HD] / out[:, HD:]).reshape(GS, TROWS, HD)
                for hh in range(GS):
                    for i in range(TILE_SY):
                        o_ref[t * TILE_SY + i, g, :, hh * HD : (hh + 1) * HD] = out[
                            hh, i * 8 : (i + 1) * 8
                        ].astype(jnp.bfloat16)

        for count in range(TILE_BLOCKS, MAXB + 1):
            pl.when(top - low + 1 == count)(functools.partial(work, count))
        return carry

    lax.fori_loop(0, NT, tile, 0)


def attention(info, q, kvs):
    smem = pl.BlockSpec(memory_space=pltpu.SMEM)
    vmem = pl.BlockSpec(memory_space=pltpu.VMEM)
    return pl.pallas_call(
        attention_kernel,
        out_shape=jax.ShapeDtypeStruct((NSY, NG, ROWS, GS * HD), jnp.bfloat16),
        in_specs=[smem] + [vmem] * (1 + len(kvs)),
        out_specs=vmem,
        compiler_params=pltpu.CompilerParams(vmem_limit_bytes=24 * 1024 * 1024),
        cost_estimate=pl.CostEstimate(
            flops=1_600_000_000, bytes_accessed=7_000_000, transcendentals=4_000_000
        ),
        name="attention",
    )(info, q, *kvs)


def whole(kernel, mib, out_shape, *args):
    return pl.pallas_call(
        kernel,
        out_shape=out_shape,
        compiler_params=pltpu.CompilerParams(vmem_limit_bytes=mib * 1024 * 1024),
        name=kernel.__name__,
    )(*args)


def swap(value, axes):
    return lax.all_to_all(value, axes, split_axis=0, concat_axis=0, tiled=True)


def along_z(value, step):
    return lax.ppermute(value, "z", [(i, (i + step) % NZ) for i in range(NZ)])


def on_device(queries, keys, values, slot_order, doc_ids):
    slot = slot_order[0]
    bf16 = jnp.bfloat16
    z0 = lax.axis_index("z")

    kv_out = whole(
        kv_send_kernel, 60, jax.ShapeDtypeStruct((2, KVH, 2, 32, 2 * HD), bf16), slot, keys, values
    )
    q_out = whole(q_send_kernel, 24, jax.ShapeDtypeStruct((2, KVH, 2, 32, GS * HD), bf16), slot, queries)
    kv = swap(kv_out.reshape(NSY, 32, 2 * HD), PLANE)
    part = jax.ShapeDtypeStruct((GC * KROWS + 16, 2 * HD), bf16)
    up = list(whole(ring_kernel, 24, (part,) * CHUNKS, kv, doc_ids))
    down = list(up)
    have = [[one] for one in up]
    for step in range(NZ // 2 - 1):
        for c in range(CHUNKS):
            up[c] = along_z(up[c], 1)
            down[c] = along_z(down[c], -1)
            have[c] += [up[c], down[c]]
    for c in range(CHUNKS):
        have[c].append(along_z(up[c], 1) if c % 2 == 0 else along_z(down[c], -1))

    _, q_out = lax.optimization_barrier((have[0][0], q_out))
    q = swap(q_out.reshape(NSY, 32, GS * HD), PLANE)
    q = q.reshape(NSY, NG, ROWS, GS, HD).transpose(1, 3, 0, 2, 4).reshape(NG, GS, KROWS, HD)

    offsets = [0, -1, 1, -2, 2, -3, 3, 4]
    places = [(z0 + o + NZ) % NZ for o in offsets]
    info = jnp.stack(places + [z0, lax.axis_index("yh") * NG]).astype(jnp.int32)
    out = attention(info, q, [one for row in have for one in row])
    got = swap(out.reshape(NSY, NG * ROWS, GS * HD), PLANE)
    got = got.reshape(2, KVH, 2, NG * ROWS, GS * HD)
    return whole(
        put_back_kernel, 24, jax.ShapeDtypeStruct((128, QH * HD), bf16), slot, got
    )


def solution(mesh):
    fine = Mesh(mesh.devices.reshape(2, NZ, 2, 4, 2), ("yl", "z", "yh", "x", "c"))
    rows = P(("yl", "z", "yh", "x", "c"), None)
    return jax.shard_map(
        on_device,
        mesh=fine,
        in_specs=(rows, rows, rows, P(("yl", "z"), ("yh", "x", "c"), None), P(("yl", "z"), None)),
        out_specs=rows,
        check_vma=False,
    )
```

time: 149 us -> 116 us (0.78)
  waiting for transfers between devices: 45.1 us -> 30.5 us
  starting transfers between devices: 51 us -> 37.6 us
  Pallas kernels: 24.2 us -> 16.1 us
  blocking collectives: 22.3 us -> 29.5 us
  local copies, waits for them, and re-layouts: 5.01 us -> 1.76 us
    all_to_all x4 -> x2, starting transfers between devices: 33.8 us -> 14.5 us  [swap(): return lax.all_to_all(value, axes, split_axis=0, concat_axis=0, tiled=True)]
    ppermute x14, waiting for transfers between devices: 32.7 us -> 21.3 us  [along_z(): return lax.ppermute(value, 'z', [(i, (i + step) % NZ) for i in range(NZ)])]
    pallas_call x2 -> x1, Pallas kernels: 19.9 us -> 10.6 us  [attention(): pl.pallas_call(attention_kernel, out_shape=jax.ShapeDtypeStruct((NSY, NG,...]
    all_to_all x1, blocking collectives: 22.3 us -> 29.5 us  [swap(): return lax.all_to_all(value, axes, split_axis=0, concat_axis=0, tiled=True)]
    ppermute x14, starting transfers between devices: 17.3 us -> 23 us  [along_z(): return lax.ppermute(value, 'z', [(i, (i + step) % NZ) for i in range(NZ)])]
    all_to_all x4 -> x2, waiting for transfers between devices: 12.4 us -> 9.22 us  [swap(): return lax.all_to_all(value, axes, split_axis=0, concat_axis=0, tiled=True)]
    unnamed x10 -> x6, local copies, waits for them, and re-layouts: 2.56 us -> 0.01 us
    pallas_call x3 -> x4, Pallas kernels: 4.29 us -> 5.54 us  [whole(): pl.pallas_call(kernel, out_shape=out_shape, compiler_params=pltpu.Compile...]
  transfers between devices with their start and end apart: 18 -> 16, of which waited for: 9 -> 10; matrix products, arithmetic and copies ran while one was open for 1% -> 2% of each run, Pallas kernels for 15% -> 1%
where the time goes in v2:
time: 116 us; the launch traced here: 115 us
  starting transfers between devices  37.6 us (32%)
  waiting for transfers between devices  30.5 us (26%)
  blocking collectives  29.5 us (25%)
  Pallas kernels  16.1 us (14%)
  local copies, waits for them, and re-layouts  1.76 us (2%)
    all_to_all x1, blocking collectives, swap(): return lax.all_to_all(value, axes, split_axis=0, concat_axis=0, tiled=True)  29.5 us
    ppermute x14, starting transfers between devices, along_z(): return lax.ppermute(value, 'z', [(i, (i + step) % NZ) for i in range(NZ)])  23 us
    ppermute x14, waiting for transfers between devices, along_z(): return lax.ppermute(value, 'z', [(i, (i + step) % NZ) for i in range(NZ)])  21.3 us
    all_to_all x2, starting transfers between devices, swap(): return lax.all_to_all(value, axes, split_axis=0, concat_axis=0, tiled=True)  14.5 us
    pallas_call x1, Pallas kernels, attention(): pl.pallas_call(attention_kernel, out_shape=jax.ShapeDtypeStruct((NSY, NG,...  10.6 us
    all_to_all x2, waiting for transfers between devices, swap(): return lax.all_to_all(value, axes, split_axis=0, concat_axis=0, tiled=True)  9.22 us
    pallas_call x4, Pallas kernels, whole(): pl.pallas_call(kernel, out_shape=out_shape, compiler_params=pltpu.Compile...  5.54 us
  transfers between devices with their start and end apart: 16, of which 10 were waited for; matrix products, arithmetic and copies ran while one was open for 2% of the time, Pallas kernels for 1%

profile of v2, /device:TPU:1, one launch (start us, length us, event | category | flops | bytes accessed | tf_op | source)
XLA Modules:
  0.0 115.5 jit_solution(2490137987922822828)
XLA Ops:
  0.0 2.3 %kv_send_kernel.1 = bf16[2,8,2,32,256]{4,3,2,1,0:T(8,128)(2,1)} custom-call(s32[1,128]{1,0:T(1,128)} %bitcast.24, bf16[128,1024]{1,0:T(8,128)(2,1)} %k_ref.1, bf16[128,1024]{1,0:T(8,128)(2,1)} %v_ref.1), custom_call_target="tpu_custom_call" | custom-call | tf_op jit(solution)/shard_map/kv_send_kernel/pallas_call | solution.py:187
  2.3 8.6 %all-to-all-start = ((bf16[32,32,256]{2,1,0:T(8,128)(2,1)}), bf16[32,32,256]{2,1,0:T(8,128)(2,1)S(1)}, u32[]{:S(2)}, u32[]{:S(2)}) async-start(bf16[32,32,256]{2,1,0:T(8,128)(2,1)} %bitcast.27), calls=%async_computation | async-start | bytes 1048576 | tf_op jit(solution)/shard_map/all_to_all | solution.py:196
  10.9 0.0 copy-start.1
  10.9 1.6 %q_send_kernel.1 = bf16[2,8,2,32,640]{4,3,2,1,0:T(8,128)(2,1)} custom-call(s32[1,128]{1,0:T(1,128)S(1)} %bitcast.25, bf16[128,5120]{1,0:T(8,128)(2,1)S(1)} %copy-done), custom_call_target="tpu_custom_call" | custom-call | tf_op jit(solution)/shard_map/q_send_kernel/pallas_call | solution.py:187
  12.5 9.2 %all-to-all-done.kv_ref = bf16[32,32,256]{2,1,0:T(8,128)(2,1)S(1)} async-done(((bf16[32,32,256]{2,1,0:T(8,128)(2,1)}), bf16[32,32,256]{2,1,0:T(8,128)(2,1)S(1)}, u32[]{:S(2)}, u32[]{:S(2)}) %all-to-all-start) | async-done | bytes 524320 | tf_op jit(solution)/shard_map/all_to_all | solution.py:196
  21.7 0.1 ring_kernel.1
  21.8 6.0 %all-to-all-start.1 = ((bf16[32,32,640]{2,1,0:T(8,128)(2,1)}), bf16[32,32,640]{2,1,0:T(8,128)(2,1)}, u32[]{:S(2)}, u32[]{:S(2)}) async-start(bf16[32,32,640]{2,1,0:T(8,128)(2,1)} %bitcast.12), calls=%async_computation.1 | async-start | bytes 2621440 | tf_op jit(solution)/shard_map/all_to_all | solution.py:196
  27.8 1.7 %collective-permute-start = (bf16[528,256]{1,0:T(8,128)(2,1)S(1)}, bf16[528,256]{1,0:T(8,128)(2,1)S(1)}, u32[]{:S(2)}, u32[]{:S(2)}) collective-permute-start(bf16[528,256]{1,0:T(8,128)(2,1)S(1)} %get-tuple-element.8.refs_0_), channel_id=1, source_target_pairs={{0,16},{16,32},{32,48},{48,64},{64,80},{80,96},{96,112},{112,0},{1... | collective-permute-start | bytes 811016 | tf_op jit(solution)/shard_map/ppermute | solution.py:200
  29.5 4.0 %collective-permute-start.8 = (bf16[528,256]{1,0:T(8,128)(2,1)S(1)}, bf16[528,256]{1,0:T(8,128)(2,1)S(1)}, u32[]{:S(2)}, u32[]{:S(2)}) collective-permute-start(bf16[528,256]{1,0:T(8,128)(2,1)S(1)} %get-tuple-element.10.refs_8_), channel_id=1, source_target_pairs={{0,112},{16,0},{32,16},{48,32},{64,48},{80,64},{96,80},{112,96},{1... | collective-permute-start | bytes 811016 | tf_op jit(solution)/shard_map/ppermute | solution.py:200
  33.6 1.4 %collective-permute-start.1 = (bf16[528,256]{1,0:T(8,128)(2,1)S(1)}, bf16[528,256]{1,0:T(8,128)(2,1)S(1)}, u32[]{:S(2)}, u32[]{:S(2)}) collective-permute-start(bf16[528,256]{1,0:T(8,128)(2,1)S(1)} %get-tuple-element.8.refs_0_), channel_id=1, source_target_pairs={{0,112},{16,0},{32,16},{48,32},{64,48},{80,64},{96,80},{112,96},{1... | collective-permute-start | bytes 811016 | tf_op jit(solution)/shard_map/ppermute | solution.py:200
  34.9 0.1 collective-permute-start.7
  35.0 5.1 %collective-permute-done.refs_1_ = bf16[528,256]{1,0:T(8,128)(2,1)S(1)} collective-permute-done((bf16[528,256]{1,0:T(8,128)(2,1)S(1)}, bf16[528,256]{1,0:T(8,128)(2,1)S(1)}, u32[]{:S(2)}, u32[]{:S(2)}) %collective-permute-start) | collective-permute-done | bytes 270368 | tf_op jit(solution)/shard_map/ppermute | solution.py:200
  40.1 0.0 collective-permute-start.2
  40.1 0.0 collective-permute-done.8.refs_10_
  40.1 2.7 %collective-permute-start.10 = (bf16[528,256]{1,0:T(8,128)(2,1)S(1)}, bf16[528,256]{1,0:T(8,128)(2,1)S(1)}, u32[]{:S(2)}, u32[]{:S(2)}) collective-permute-start(bf16[528,256]{1,0:T(8,128)(2,1)S(1)} %collective-permute-done.8.refs_10_), channel_id=1, source_target_pairs={{0,112},{16,0},{32,16},{48,32},{64,48},{80,64},{96,80},{112,96},{1... | collective-permute-start | bytes 811016 | tf_op jit(solution)/shard_map/ppermute | solution.py:200
  42.8 2.0 %collective-permute-done.1.refs_2_ = bf16[528,256]{1,0:T(8,128)(2,1)S(1)} collective-permute-done((bf16[528,256]{1,0:T(8,128)(2,1)S(1)}, bf16[528,256]{1,0:T(8,128)(2,1)S(1)}, u32[]{:S(2)}, u32[]{:S(2)}) %collective-permute-start.1) | collective-permute-done | bytes 270368 | tf_op jit(solution)/shard_map/ppermute | solution.py:200
  44.8 3.5 %collective-permute-start.3 = (bf16[528,256]{1,0:T(8,128)(2,1)S(1)}, bf16[528,256]{1,0:T(8,128)(2,1)S(1)}, u32[]{:S(2)}, u32[]{:S(2)}) collective-permute-start(bf16[528,256]{1,0:T(8,128)(2,1)S(1)} %collective-permute-done.1.refs_2_), channel_id=1, source_target_pairs={{0,112},{16,0},{32,16},{48,32},{64,48},{80,64},{96,80},{112,96},{1... | collective-permute-start | bytes 811016 | tf_op jit(solution)/shard_map/ppermute | solution.py:200
  48.3 3.2 %collective-permute-done.2.refs_3_ = bf16[528,256]{1,0:T(8,128)(2,1)S(1)} collective-permute-done((bf16[528,256]{1,0:T(8,128)(2,1)S(1)}, bf16[528,256]{1,0:T(8,128)(2,1)S(1)}, u32[]{:S(2)}, u32[]{:S(2)}) %collective-permute-start.2) | collective-permute-done | bytes 270368 | tf_op jit(solution)/shard_map/ppermute | solution.py:200
  51.6 2.7 %collective-permute-start.12 = (bf16[528,256]{1,0:T(8,128)(2,1)S(1)}, bf16[528,256]{1,0:T(8,128)(2,1)}, u32[]{:S(2)}, u32[]{:S(2)}) collective-permute-start(bf16[528,256]{1,0:T(8,128)(2,1)S(1)} %collective-permute-done.10.refs_12_), channel_id=1, source_target_pairs={{0,112},{16,0},{32,16},{48,32},{64,48},{80,64},{96,80},{112,96},{1... | collective-permute-start | bytes 811016 | tf_op jit(solution)/shard_map/ppermute | solution.py:200
  54.2 0.1 stack.43.info_ref
  54.3 2.1 %collective-permute-done.3.refs_4_ = bf16[528,256]{1,0:T(8,128)(2,1)S(1)} collective-permute-done((bf16[528,256]{1,0:T(8,128)(2,1)S(1)}, bf16[528,256]{1,0:T(8,128)(2,1)S(1)}, u32[]{:S(2)}, u32[]{:S(2)}) %collective-permute-start.3) | collective-permute-done | bytes 270368 | tf_op jit(solution)/shard_map/ppermute | solution.py:200
  56.4 3.4 %collective-permute-start.5 = (bf16[528,256]{1,0:T(8,128)(2,1)S(1)}, bf16[528,256]{1,0:T(8,128)(2,1)}, u32[]{:S(2)}, u32[]{:S(2)}) collective-permute-start(bf16[528,256]{1,0:T(8,128)(2,1)S(1)} %collective-permute-done.3.refs_4_), channel_id=1, source_target_pairs={{0,112},{16,0},{32,16},{48,32},{64,48},{80,64},{96,80},{112,96},{1... | collective-permute-start | bytes 811016 | tf_op jit(solution)/shard_map/ppermute | solution.py:200
  59.8 1.4 %collective-permute-done.4.refs_5_ = bf16[528,256]{1,0:T(8,128)(2,1)S(1)} collective-permute-done((bf16[528,256]{1,0:T(8,128)(2,1)S(1)}, bf16[528,256]{1,0:T(8,128)(2,1)S(1)}, u32[]{:S(2)}, u32[]{:S(2)}) %collective-permute-start.4) | collective-permute-done | bytes 270368 | tf_op jit(solution)/shard_map/ppermute | solution.py:200
  61.2 1.0 collective-permute-done.12.refs_14_
  62.2 3.5 %collective-permute-start.13 = (bf16[528,256]{1,0:T(8,128)(2,1)}, bf16[528,256]{1,0:T(8,128)(2,1)}, u32[]{:S(2)}, u32[]{:S(2)}) collective-permute-start(bf16[528,256]{1,0:T(8,128)(2,1)} %collective-permute-done.12.refs_14_), channel_id=1, source_target_pairs={{0,112},{16,0},{32,16},{48,32},{64,48},{80,64},{96,80},{112,96},{1... | collective-permute-start | bytes 811016 | tf_op jit(solution)/shard_map/ppermute | solution.py:200
  65.7 1.7 %copy_bitcast_fusion.q_ref = bf16[4,5,256,128]{3,2,1,0:T(8,128)(2,1)S(1)} fusion(bf16[32,32,640]{2,1,0:T(8,128)(2,1)} %all-to-all-done.1), kind=kLoop, calls=%fused_computation | loop fusion | bytes 2621440 | tf_op jit(solution)/shard_map/reshape | solution.py:227
  67.4 0.6 collective-permute-done.5.refs_6_
  68.0 4.7 %collective-permute-done.6.refs_7_ = bf16[528,256]{1,0:T(8,128)(2,1)} collective-permute-done((bf16[528,256]{1,0:T(8,128)(2,1)S(1)}, bf16[528,256]{1,0:T(8,128)(2,1)}, u32[]{:S(2)}, u32[]{:S(2)}) %collective-permute-start.6) | collective-permute-done | bytes 270368 | tf_op jit(solution)/shard_map/ppermute | solution.py:200
  72.7 1.1 collective-permute-done.13.refs_15_
  73.9 10.6 %attention.1 = bf16[32,4,8,640]{3,2,1,0:T(8,128)(2,1)S(1)} custom-call(s32[10]{0:T(128)S(1)} %stack.43.info_ref, bf16[4,5,256,128]{3,2,1,0:T(8,128)(2,1)S(1)} %copy_bitcast_fusion.q_ref, bf16[528,256]{1,0:T(8,128)(2,1)S(1)} %get-tuple-element.8.refs_0_, bf16[528,256]{1,0:T(8,128)(2,1)S(1)} %collective-permute-done.refs_1_, ...), custom_call_target="tpu_custom_call" | custom-call | flops 1600000000 | bytes 7000000 | tf_op jit(solution)/shard_map/attention/pallas_call | solution.py:173
  84.4 29.5 %all_to_all.15 = bf16[32,32,640]{2,1,0:T(8,128)(2,1)S(1)} all-to-all(bf16[32,32,640]{2,1,0:T(8,128)(2,1)S(1)} %bitcast.23), channel_id=1, replica_groups=mesh['yl'=2,'z'=8,'yh'=2,'x'=4,'c'=2] {'yh','x','c','yl'}, dimensions={0} | all-to-all | bytes 2621440 | tf_op jit(solution)/shard_map/all_to_all | solution.py:196
  113.9 1.5 %put_back_kernel.1 = bf16[128,5120]{1,0:T(8,128)(2,1)} custom-call(s32[1,128]{1,0:T(1,128)S(1)} %bitcast.26, bf16[2,8,2,32,640]{4,3,2,1,0:T(8,128)(2,1)S(1)} %bitcast.22), custom_call_target="tpu_custom_call" | custom-call | tf_op jit(solution)/shard_map/put_back_kernel/pallas_call | solution.py:187
  (14 shorter events, 0.0 us)
Async XLA Ops:
  0.0 10.9 %copy-start.2 = (s32[1,1,128]{2,1,0:T(1,128)S(1)}, s32[1,1,128]{2,1,0:T(1,128)}, u32[]{:S(2)}) copy-start(s32[1,1,128]{2,1,0:T(1,128)} %param.8) | copy-start | bytes 1540
  0.0 10.9 %copy-start = (bf16[128,5120]{1,0:T(8,128)(2,1)S(1)}, bf16[128,5120]{1,0:T(8,128)(2,1)}, u32[]{:S(2)}) copy-start(bf16[128,5120]{1,0:T(8,128)(2,1)} %q_ref.1) | copy-start | bytes 3932164
  2.3 19.4 %all-to-all-start = ((bf16[32,32,256]{2,1,0:T(8,128)(2,1)}), bf16[32,32,256]{2,1,0:T(8,128)(2,1)S(1)}, u32[]{:S(2)}, u32[]{:S(2)}) async-start(bf16[32,32,256]{2,1,0:T(8,128)(2,1)} %bitcast.27), calls=%async_computation | async-start | bytes 1048576 | tf_op jit(solution)/shard_map/all_to_all | solution.py:196
  10.9 10.8 %copy-start.1 = (s32[1,2048]{1,0:T(1,128)S(1)}, s32[1,2048]{1,0:T(1,128)}, u32[]{:S(2)}) copy-start(s32[1,2048]{1,0:T(1,128)} %doc_ref.1) | copy-start | bytes 24580
  21.8 43.9 %all-to-all-start.1 = ((bf16[32,32,640]{2,1,0:T(8,128)(2,1)}), bf16[32,32,640]{2,1,0:T(8,128)(2,1)}, u32[]{:S(2)}, u32[]{:S(2)}) async-start(bf16[32,32,640]{2,1,0:T(8,128)(2,1)} %bitcast.12), calls=%async_computation.1 | async-start | bytes 2621440 | tf_op jit(solution)/shard_map/all_to_all | solution.py:196
  27.8 12.3 %collective-permute-start = (bf16[528,256]{1,0:T(8,128)(2,1)S(1)}, bf16[528,256]{1,0:T(8,128)(2,1)S(1)}, u32[]{:S(2)}, u32[]{:S(2)}) collective-permute-start(bf16[528,256]{1,0:T(8,128)(2,1)S(1)} %get-tuple-element.8.refs_0_), channel_id=1, source_target_pairs={{0,16},{16,32},{32,48},{48,64},{64,80},{80,96},{96,112},{112,0},{1... | collective-permute-start | bytes 811016 | tf_op jit(solution)/shard_map/ppermute | solution.py:200
  29.5 10.6 %collective-permute-start.8 = (bf16[528,256]{1,0:T(8,128)(2,1)S(1)}, bf16[528,256]{1,0:T(8,128)(2,1)S(1)}, u32[]{:S(2)}, u32[]{:S(2)}) collective-permute-start(bf16[528,256]{1,0:T(8,128)(2,1)S(1)} %get-tuple-element.10.refs_8_), channel_id=1, source_target_pairs={{0,112},{16,0},{32,16},{48,32},{64,48},{80,64},{96,80},{112,96},{1... | collective-permute-start | bytes 811016 | tf_op jit(solution)/shard_map/ppermute | solution.py:200
  33.6 11.2 %collective-permute-start.1 = (bf16[528,256]{1,0:T(8,128)(2,1)S(1)}, bf16[528,256]{1,0:T(8,128)(2,1)S(1)}, u32[]{:S(2)}, u32[]{:S(2)}) collective-permute-start(bf16[528,256]{1,0:T(8,128)(2,1)S(1)} %get-tuple-element.8.refs_0_), channel_id=1, source_target_pairs={{0,112},{16,0},{32,16},{48,32},{64,48},{80,64},{96,80},{112,96},{1... | collective-permute-start | bytes 811016 | tf_op jit(solution)/shard_map/ppermute | solution.py:200
  34.9 13.4 %collective-permute-start.7 = (bf16[528,256]{1,0:T(8,128)(2,1)S(1)}, bf16[528,256]{1,0:T(8,128)(2,1)S(1)}, u32[]{:S(2)}, u32[]{:S(2)}) collective-permute-start(bf16[528,256]{1,0:T(8,128)(2,1)S(1)} %get-tuple-element.10.refs_8_), channel_id=1, source_target_pairs={{0,16},{16,32},{32,48},{48,64},{64,80},{80,96},{96,112},{112,0},{1... | collective-permute-start | bytes 811016 | tf_op jit(solution)/shard_map/ppermute | solution.py:200
  40.1 11.5 %collective-permute-start.2 = (bf16[528,256]{1,0:T(8,128)(2,1)S(1)}, bf16[528,256]{1,0:T(8,128)(2,1)S(1)}, u32[]{:S(2)}, u32[]{:S(2)}) collective-permute-start(bf16[528,256]{1,0:T(8,128)(2,1)S(1)} %collective-permute-done.refs_1_), channel_id=1, source_target_pairs={{0,16},{16,32},{32,48},{48,64},{64,80},{80,96},{96,112},{112,0},{1... | collective-permute-start | bytes 811016 | tf_op jit(solution)/shard_map/ppermute | solution.py:200
  40.1 11.5 %collective-permute-start.10 = (bf16[528,256]{1,0:T(8,128)(2,1)S(1)}, bf16[528,256]{1,0:T(8,128)(2,1)S(1)}, u32[]{:S(2)}, u32[]{:S(2)}) collective-permute-start(bf16[528,256]{1,0:T(8,128)(2,1)S(1)} %collective-permute-done.8.refs_10_), channel_id=1, source_target_pairs={{0,112},{16,0},{32,16},{48,32},{64,48},{80,64},{96,80},{112,96},{1... | collective-permute-start | bytes 811016 | tf_op jit(solution)/shard_map/ppermute | solution.py:200
  44.8 11.6 %collective-permute-start.3 = (bf16[528,256]{1,0:T(8,128)(2,1)S(1)}, bf16[528,256]{1,0:T(8,128)(2,1)S(1)}, u32[]{:S(2)}, u32[]{:S(2)}) collective-permute-start(bf16[528,256]{1,0:T(8,128)(2,1)S(1)} %collective-permute-done.1.refs_2_), channel_id=1, source_target_pairs={{0,112},{16,0},{32,16},{48,32},{64,48},{80,64},{96,80},{112,96},{1... | collective-permute-start | bytes 811016 | tf_op jit(solution)/shard_map/ppermute | solution.py:200
  48.3 11.5 %collective-permute-start.9 = (bf16[528,256]{1,0:T(8,128)(2,1)S(1)}, bf16[528,256]{1,0:T(8,128)(2,1)S(1)}, u32[]{:S(2)}, u32[]{:S(2)}) collective-permute-start(bf16[528,256]{1,0:T(8,128)(2,1)S(1)} %collective-permute-done.7.refs_9_), channel_id=1, source_target_pairs={{0,16},{16,32},{32,48},{48,64},{64,80},{80,96},{96,112},{112,0},{1... | collective-permute-start | bytes 811016 | tf_op jit(solution)/shard_map/ppermute | solution.py:200
  51.6 9.6 %collective-permute-start.4 = (bf16[528,256]{1,0:T(8,128)(2,1)S(1)}, bf16[528,256]{1,0:T(8,128)(2,1)S(1)}, u32[]{:S(2)}, u32[]{:S(2)}) collective-permute-start(bf16[528,256]{1,0:T(8,128)(2,1)S(1)} %collective-permute-done.2.refs_3_), channel_id=1, source_target_pairs={{0,16},{16,32},{32,48},{48,64},{64,80},{80,96},{96,112},{112,0},{1... | collective-permute-start | bytes 811016 | tf_op jit(solution)/shard_map/ppermute | solution.py:200
  51.6 10.6 %collective-permute-start.12 = (bf16[528,256]{1,0:T(8,128)(2,1)S(1)}, bf16[528,256]{1,0:T(8,128)(2,1)}, u32[]{:S(2)}, u32[]{:S(2)}) collective-permute-start(bf16[528,256]{1,0:T(8,128)(2,1)S(1)} %collective-permute-done.10.refs_12_), channel_id=1, source_target_pairs={{0,112},{16,0},{32,16},{48,32},{64,48},{80,64},{96,80},{112,96},{1... | collective-permute-start | bytes 811016 | tf_op jit(solution)/shard_map/ppermute | solution.py:200
  56.4 11.6 %collective-permute-start.5 = (bf16[528,256]{1,0:T(8,128)(2,1)S(1)}, bf16[528,256]{1,0:T(8,128)(2,1)}, u32[]{:S(2)}, u32[]{:S(2)}) collective-permute-start(bf16[528,256]{1,0:T(8,128)(2,1)S(1)} %collective-permute-done.3.refs_4_), channel_id=1, source_target_pairs={{0,112},{16,0},{32,16},{48,32},{64,48},{80,64},{96,80},{112,96},{1... | collective-permute-start | bytes 811016 | tf_op jit(solution)/shard_map/ppermute | solution.py:200
  59.8 8.2 %collective-permute-start.11 = (bf16[528,256]{1,0:T(8,128)(2,1)S(1)}, bf16[528,256]{1,0:T(8,128)(2,1)}, u32[]{:S(2)}, u32[]{:S(2)}) collective-permute-start(bf16[528,256]{1,0:T(8,128)(2,1)S(1)} %collective-permute-done.9.refs_11_), channel_id=1, source_target_pairs={{0,16},{16,32},{32,48},{48,64},{64,80},{80,96},{96,112},{112,0},{1... | collective-permute-start | bytes 811016 | tf_op jit(solution)/shard_map/ppermute | solution.py:200
  61.2 11.5 %collective-permute-start.6 = (bf16[528,256]{1,0:T(8,128)(2,1)S(1)}, bf16[528,256]{1,0:T(8,128)(2,1)}, u32[]{:S(2)}, u32[]{:S(2)}) collective-permute-start(bf16[528,256]{1,0:T(8,128)(2,1)S(1)} %collective-permute-done.4.refs_5_), channel_id=1, source_target_pairs={{0,16},{16,32},{32,48},{48,64},{64,80},{80,96},{96,112},{112,0},{1... | collective-permute-start | bytes 811016 | tf_op jit(solution)/shard_map/ppermute | solution.py:200
  62.2 11.7 %collective-permute-start.13 = (bf16[528,256]{1,0:T(8,128)(2,1)}, bf16[528,256]{1,0:T(8,128)(2,1)}, u32[]{:S(2)}, u32[]{:S(2)}) collective-permute-start(bf16[528,256]{1,0:T(8,128)(2,1)} %collective-permute-done.12.refs_14_), channel_id=1, source_target_pairs={{0,112},{16,0},{32,16},{48,32},{64,48},{80,64},{96,80},{112,96},{1... | collective-permute-start | bytes 811016 | tf_op jit(solution)/shard_map/ppermute | solution.py:200

commit v3 on v2

v3 whole, which is shorter than its diff:
```python
import functools

import jax
import jax.numpy as jnp
from jax import lax
from jax.experimental import pallas as pl
from jax.experimental.pallas import tpu as pltpu
from jax.sharding import Mesh
from jax.sharding import PartitionSpec as P

QH = 40
KVH = 8
HD = 128
GS = QH // KVH
NZ = 8
NSY = 32
NG = 4
ROWS = 8
KROWS = NSY * ROWS
CHUNKS = 2
GC = NG // CHUNKS
TILE_SY = 4
JOIN = 2
TROWS = TILE_SY * ROWS
NT = NSY // TILE_SY
TILE_POS = TILE_SY * 64
BLOCK_POS = 256
BLOCK_ROWS = BLOCK_POS // NZ
TILE_BLOCKS = TILE_POS // BLOCK_POS
MAXB = TILE_BLOCKS + 4
NEG = -1e30
SCALE = (HD**-0.5) * 1.4426950408889634
PLANE = ("yh", "x", "c", "yl")


def one_hot_t(slot):
    rows = lax.broadcasted_iota(jnp.int32, (128, 128), 0)
    return (rows == slot).astype(jnp.float32).astype(jnp.bfloat16)


def pick(onehot, x):
    return lax.dot_general(
        onehot, x, (((0,), (0,)), ((), ())), preferred_element_type=jnp.float32
    ).astype(jnp.bfloat16)


def kv_send_kernel(slot_ref, k_ref, v_ref, o_ref):
    onehot = one_hot_t(slot_ref[...])
    for part, ref in enumerate((k_ref, v_ref)):
        got = pick(onehot, ref[...])
        for h in range(KVH):
            for yl in range(2):
                for yh in range(2):
                    at = (yl * 2 + yh) * 32
                    o_ref[yh, h, yl, :, part * HD : (part + 1) * HD] = got[
                        at : at + 32, h * HD : (h + 1) * HD
                    ]


def edge_kernel(doc_ref, o_ref):
    doc = doc_ref[...]
    lane = lax.broadcasted_iota(jnp.int32, (16, HD), 1)
    out = jnp.zeros((16, HD), jnp.float32)
    for i in range(3):
        edge = jnp.sum((doc <= i).astype(jnp.int32), axis=1, keepdims=True)
        out = jnp.where(lane == 2 * i, (edge // 64).astype(jnp.float32), out)
        out = jnp.where(lane == 2 * i + 1, (edge % 64).astype(jnp.float32), out)
    o_ref[...] = out.astype(jnp.bfloat16)


def ring_kernel(kv_ref, edge_ref, far_ref, *o_refs):
    rows = [kv_ref[sy].astype(jnp.float32) for sy in range(NSY)]
    for c, o_ref in enumerate(o_refs):
        for g in range(GC):
            at = (c * GC + g) * ROWS
            part = jnp.concatenate([r[at : at + ROWS] for r in rows], axis=0)
            o_ref[g * KROWS : (g + 1) * KROWS, :] = part.astype(jnp.bfloat16)
        o_ref[GC * KROWS :, :HD] = edge_ref[...]
        o_ref[GC * KROWS :, HD:] = far_ref[...]


def q_send_kernel(slot_ref, q_ref, o_ref):
    onehot = one_hot_t(slot_ref[...])
    for h in range(KVH):
        got = pick(onehot, q_ref[:, h * GS * HD : (h + 1) * GS * HD])
        for yl in range(2):
            for yh in range(2):
                at = (yl * 2 + yh) * 32
                o_ref[yh, h, yl] = got[at : at + 32]


def put_back_kernel(slot_ref, got_ref, o_ref, buf, sems):
    onehot = one_hot_t(slot_ref[...])
    stores = []
    for h in range(KVH):
        cols = pl.ds(h * GS * HD, GS * HD)
        rows = [got_ref[yh, h, yl] for yl in range(2) for yh in range(2)]
        back = jnp.dot(onehot, jnp.concatenate(rows, axis=0), preferred_element_type=jnp.float32)
        buf[:, cols] = back.astype(jnp.bfloat16)
        stores.append(pltpu.make_async_copy(buf.at[:, cols], o_ref.at[:, cols], sems.at[h]))
        stores[-1].start()
    for store in stores:
        store.wait()


def doc_start(pos, inner):
    b1, b2, b3 = inner
    return jnp.where(pos >= b3, b3, jnp.where(pos >= b2, b2, jnp.where(pos >= b1, b1, 0)))


def edges_of(info_ref, refs):
    tails = [r[GC * KROWS :, :HD].astype(jnp.float32) for r in refs[: NZ - 1]]
    tails.append(refs[0][GC * KROWS :, HD:].astype(jnp.float32))
    inner = []
    for gg in range(NG):
        mine = jnp.zeros_like(tails[0])
        for i in range(NZ):
            mine = jnp.where(info_ref[i] == info_ref[NZ + 1] + gg, tails[i], mine)
        found = [mine[0, lane].astype(jnp.int32) for lane in range(6)]
        inner.append([found[2 * i] * 64 + found[2 * i + 1] for i in range(3)])
    return inner


def near_kernel(chunk, info_ref, edge_in, q_ref, *refs):
    per = NZ - 1
    kv_refs = refs[:per]
    m_ref, acc_ref = refs[per : per + 2]
    z0 = info_ref[NZ]
    q_iota = lax.broadcasted_iota(jnp.int32, (TROWS, 1), 0)
    q_rel = (q_iota // 8) * 64 + q_iota % 8 + z0 * 8
    if chunk == 0:
        every = edges_of(info_ref, kv_refs)
        for g in range(NG):
            for i in range(3):
                refs[per + 2][g, i] = every[g][i]
    else:
        every = [[edge_in[g, i] for i in range(3)] for g in range(NG)]
    inner = every[chunk * GC : (chunk + 1) * GC]

    def tiles(u, carry):
        count_of = None
        for j in range(JOIN):
            t = u * JOIN + j
            first_pos = t * TILE_POS + z0 * 8
            for g in range(GC):
                low = doc_start(first_pos, inner[g]) // BLOCK_POS
                need = (t + 1) * TILE_BLOCKS - low
                count_of = need if count_of is None else jnp.maximum(count_of, need)

        def work(count):
            rows = count * BLOCK_ROWS
            width = -(-per * rows // 128) * 128
            col = lax.broadcasted_iota(jnp.int32, (1, width), 1)
            inside, k_z = col, jnp.full_like(col, info_ref[0])
            for i in range(1, per):
                inside = jnp.where(col >= i * rows, col - i * rows, inside)
                k_z = jnp.where(col >= i * rows, info_ref[i], k_z)
            k_rel = (inside // 8) * 64 + inside % 8 + k_z * 8
            k_rel = jnp.where(col >= per * rows, 1 << 20, k_rel)
            pad = [jnp.zeros((width - per * rows, HD), jnp.bfloat16)] * (width > per * rows)
            items, scores, vals = [], [], []
            for j in range(JOIN):
                t = u * JOIN + j
                row0 = pl.multiple_of(t * TROWS, TROWS)
                block = jnp.maximum((t + 1) * TILE_BLOCKS - count, 0)
                for g in range(GC):
                    q_tile = q_ref[chunk * GC + g, :, pl.ds(row0, TROWS), :]
                    k0 = pl.multiple_of(g * KROWS + block * BLOCK_ROWS, BLOCK_ROWS)
                    at = pl.ds(k0, rows)
                    keys = jnp.concatenate([r[at, :HD] for r in kv_refs] + pad, axis=0)
                    val = jnp.concatenate([r[at, HD:] for r in kv_refs] + pad, axis=0)
                    vals.append(jnp.concatenate([val, jnp.ones_like(val)], axis=1))
                    s = lax.dot_general(
                        q_tile.reshape(GS * TROWS, HD),
                        keys,
                        (((1,), (1,)), ((), ())),
                        preferred_element_type=jnp.float32,
                    )
                    k_pos = block * BLOCK_POS + k_rel
                    q_pos = t * TILE_POS + q_rel
                    ok = (k_pos <= q_pos) & (k_pos >= doc_start(q_pos, inner[g]))
                    bias = jnp.where(ok, 0.0, NEG)
                    scores.append(s.reshape(GS, TROWS, width) + bias[None])
                    items.append((g, row0))
            tops = [jnp.max(s, axis=-1, keepdims=True) for s in scores]
            weights = [
                jnp.exp2((s - m) * SCALE).astype(jnp.bfloat16).reshape(GS * TROWS, width)
                for s, m in zip(scores, tops)
            ]
            outs = [
                jnp.dot(w, v, preferred_element_type=jnp.float32) for w, v in zip(weights, vals)
            ]
            for (g, row0), top, out in zip(items, tops, outs):
                at = pl.ds(row0, TROWS)
                acc_ref[g, :, at, :] = out.reshape(GS, TROWS, 2 * HD)
                m_ref[g, :, at, :] = jnp.broadcast_to(top, (GS, TROWS, HD))

        for count in range(TILE_BLOCKS, MAXB + 1):
            pl.when(count_of == count)(functools.partial(work, count))
        return carry

    lax.fori_loop(0, NT // JOIN, tiles, 0)


def far_kernel(info_ref, edge_ref, q_ref, *refs):
    m_refs, acc_refs, kv_refs = (refs[i * CHUNKS : (i + 1) * CHUNKS] for i in range(3))
    o_ref = refs[3 * CHUNKS]
    r_iota = lax.broadcasted_iota(jnp.int32, (KROWS, 1), 0)
    c_iota = lax.broadcasted_iota(jnp.int32, (1, KROWS), 1)
    q_pos = (r_iota // 8) * 64 + r_iota % 8 + info_ref[NZ] * 8
    k_pos = (c_iota // 8) * 64 + c_iota % 8 + info_ref[NZ - 1] * 8
    for g in range(NG):
        q_start = doc_start(q_pos, [edge_ref[g, i] for i in range(3)])
        bias = jnp.where((k_pos <= q_pos) & (k_pos >= q_start), 0.0, NEG)
        at = pl.ds(g % GC * KROWS, KROWS)
        keys, val = kv_refs[g // GC][at, :HD], kv_refs[g // GC][at, HD:]
        val = jnp.concatenate([val, jnp.ones_like(val)], axis=1)
        for hh in range(GS):
            s = lax.dot_general(
                q_ref[g, hh], keys, (((1,), (1,)), ((), ())), preferred_element_type=jnp.float32
            )
            s = s + bias
            before = m_refs[g // GC][g % GC, hh]
            m = jnp.maximum(before, jnp.max(s, axis=-1, keepdims=True))
            w = jnp.exp2((s - jnp.concatenate([m, m], axis=1)) * SCALE).astype(jnp.bfloat16)
            out = jnp.dot(w, val, preferred_element_type=jnp.float32)
            fade = jnp.exp2((before - m) * SCALE)
            acc = acc_refs[g // GC][g % GC, hh]
            num = acc[:, :HD] * fade + out[:, :HD]
            den = acc[:, HD:] * fade + out[:, HD:]
            o_ref[:, g, :, hh * HD : (hh + 1) * HD] = (
                (num / den).reshape(NSY, ROWS, HD).astype(jnp.bfloat16)
            )


def attention_near(chunk, info, edges, q, kvs):
    smem = pl.BlockSpec(memory_space=pltpu.SMEM)
    vmem = pl.BlockSpec(memory_space=pltpu.VMEM)
    out_shape = [
        jax.ShapeDtypeStruct((GC, GS, KROWS, HD), jnp.float32),
        jax.ShapeDtypeStruct((GC, GS, KROWS, 2 * HD), jnp.float32),
    ]
    out_specs = [vmem, vmem]
    if chunk == 0:
        out_shape.append(jax.ShapeDtypeStruct((NG, 3), jnp.int32))
        out_specs.append(smem)
    return pl.pallas_call(
        functools.partial(near_kernel, chunk),
        out_shape=out_shape,
        in_specs=[smem, smem] + [vmem] * (1 + len(kvs)),
        out_specs=out_specs,
        compiler_params=pltpu.CompilerParams(vmem_limit_bytes=24 * 1024 * 1024),
        cost_estimate=pl.CostEstimate(
            flops=800_000_000, bytes_accessed=10_000_000, transcendentals=2_000_000
        ),
        name="attention_near",
    )(info, edges, q, *kvs)


def attention_far(info, edges, q, *kvs):
    smem = pl.BlockSpec(memory_space=pltpu.SMEM)
    vmem = pl.BlockSpec(memory_space=pltpu.VMEM)
    return pl.pallas_call(
        far_kernel,
        out_shape=jax.ShapeDtypeStruct((NSY, NG, ROWS, GS * HD), jnp.bfloat16),
        in_specs=[smem, smem] + [vmem] * (1 + len(kvs)),
        out_specs=vmem,
        compiler_params=pltpu.CompilerParams(vmem_limit_bytes=24 * 1024 * 1024),
        cost_estimate=pl.CostEstimate(
            flops=800_000_000, bytes_accessed=7_000_000, transcendentals=1_500_000
        ),
        name="attention_far",
    )(info, edges, q, *kvs)


def whole(kernel, mib, out_shape, *args):
    return pl.pallas_call(
        kernel,
        out_shape=out_shape,
        compiler_params=pltpu.CompilerParams(vmem_limit_bytes=mib * 1024 * 1024),
        name=kernel.__name__,
    )(*args)


def swap(value, axes):
    return lax.all_to_all(value, axes, split_axis=0, concat_axis=0, tiled=True)


def along_z(value, step):
    return lax.ppermute(value, "z", [(i, (i + step) % NZ) for i in range(NZ)])


def on_device(queries, keys, values, slot_order, doc_ids):
    slot = slot_order[0]
    bf16 = jnp.bfloat16
    z0 = lax.axis_index("z")

    kv_out = whole(
        kv_send_kernel, 60, jax.ShapeDtypeStruct((2, KVH, 2, 32, 2 * HD), bf16), slot, keys, values
    )
    q_out = whole(q_send_kernel, 24, jax.ShapeDtypeStruct((2, KVH, 2, 32, GS * HD), bf16), slot, queries)
    kv = swap(kv_out.reshape(NSY, 32, 2 * HD), PLANE)
    _, doc_ids = lax.optimization_barrier((kv_out, doc_ids))
    edge = whole(edge_kernel, 24, jax.ShapeDtypeStruct((16, HD), bf16), doc_ids)
    part = jax.ShapeDtypeStruct((GC * KROWS + 16, 2 * HD), bf16)
    up = list(whole(ring_kernel, 24, (part,) * CHUNKS, kv, edge, along_z(edge, NZ // 2)))
    down = list(up)
    have = [[one] for one in up]
    for step in range(NZ // 2 - 1):
        for c in range(CHUNKS):
            up[c] = along_z(up[c], 1)
            down[c] = along_z(down[c], -1)
            have[c] += [up[c], down[c]]
    _, q_out = lax.optimization_barrier((have[0][0], q_out))
    q = swap(q_out.reshape(NSY, 32, GS * HD), PLANE)
    q = q.reshape(NSY, NG, ROWS, GS, HD).transpose(1, 3, 0, 2, 4).reshape(NG, GS, KROWS, HD)

    offsets = [0, -1, 1, -2, 2, -3, 3, 4]
    places = [(z0 + o + NZ) % NZ for o in offsets]
    info = jnp.stack(places + [z0, lax.axis_index("yh") * NG]).astype(jnp.int32)
    last = [along_z(up[0], 1), along_z(down[1], -1)]
    m0, acc0, edges = attention_near(0, info, info[None], q, have[0])
    m1, acc1 = attention_near(1, info, edges, q, have[1])
    out = attention_far(info, edges, q, m0, m1, acc0, acc1, *last)
    got = swap(out.reshape(NSY, NG * ROWS, GS * HD), PLANE)
    got = got.reshape(2, KVH, 2, NG * ROWS, GS * HD)
    vmem = pl.BlockSpec(memory_space=pltpu.VMEM)
    return pl.pallas_call(
        put_back_kernel,
        out_shape=jax.ShapeDtypeStruct((128, QH * HD), bf16),
        in_specs=[vmem, vmem],
        out_specs=pl.BlockSpec(memory_space=pltpu.HBM),
        scratch_shapes=[pltpu.VMEM((128, QH * HD), bf16), pltpu.SemaphoreType.DMA((KVH,))],
        compiler_params=pltpu.CompilerParams(vmem_limit_bytes=24 * 1024 * 1024),
        name="put_back",
    )(slot, got)


def solution(mesh):
    fine = Mesh(mesh.devices.reshape(2, NZ, 2, 4, 2), ("yl", "z", "yh", "x", "c"))
    rows = P(("yl", "z", "yh", "x", "c"), None)
    return jax.shard_map(
        on_device,
        mesh=fine,
        in_specs=(rows, rows, rows, P(("yl", "z"), ("yh", "x", "c"), None), P(("yl", "z"), None)),
        out_specs=rows,
        check_vma=False,
    )
```

time: 116 us -> 114 us (0.983)
  waiting for transfers between devices: 30.5 us -> 17.5 us
  starting transfers between devices: 37.6 us -> 44.6 us
  Pallas kernels: 16.1 us -> 20.6 us
    all_to_all x2, waiting for transfers between devices: 9.22 us -> 2.11 us  [swap(): return lax.all_to_all(value, axes, split_axis=0, concat_axis=0, tiled=True)]
    ppermute x14 -> x15, starting transfers between devices: 23 us -> 30 us  [along_z(): return lax.ppermute(value, 'z', [(i, (i + step) % NZ) for i in range(NZ)])]
    pallas_call x1 -> x4, Pallas kernels: 10.6 us -> 16.6 us  [the longest x2 11.9 us: attention_near(): pl.pallas_call(functools.partial(near_kernel, chunk), out_shape=out_shape...]
    ppermute x14 -> x15, waiting for transfers between devices: 21.3 us -> 15.4 us  [along_z(): return lax.ppermute(value, 'z', [(i, (i + step) % NZ) for i in range(NZ)])]
    pallas_call x4, Pallas kernels: 5.54 us -> 4.03 us  [whole(): pl.pallas_call(kernel, out_shape=out_shape, compiler_params=pltpu.Compile...]
  transfers between devices with their start and end apart: 16 -> 17, of which waited for: 10 -> 8; matrix products, arithmetic and copies ran while one was open for 2% -> 2% of each run, Pallas kernels for 1% -> 12%
where the time goes in v3:
time: 114 us
  starting transfers between devices  44.6 us (39%)
  blocking collectives  29.1 us (26%)
  Pallas kernels  20.6 us (18%)
  waiting for transfers between devices  17.5 us (15%)
  local copies, waits for them, and re-layouts  1.75 us (2%)
    ppermute x15, starting transfers between devices, along_z(): return lax.ppermute(value, 'z', [(i, (i + step) % NZ) for i in range(NZ)])  30 us
    all_to_all x1, blocking collectives, swap(): return lax.all_to_all(value, axes, split_axis=0, concat_axis=0, tiled=True)  29.1 us
    ppermute x15, waiting for transfers between devices, along_z(): return lax.ppermute(value, 'z', [(i, (i + step) % NZ) for i in range(NZ)])  15.4 us
    all_to_all x2, starting transfers between devices, swap(): return lax.all_to_all(value, axes, split_axis=0, concat_axis=0, tiled=True)  14.6 us
    pallas_call x2, Pallas kernels, attention_near(): pl.pallas_call(functools.partial(near_kernel, chunk), out_shape=out_shape...  11.9 us
    pallas_call x4, Pallas kernels, whole(): pl.pallas_call(kernel, out_shape=out_shape, compiler_params=pltpu.Compile...  4.03 us
    pallas_call x1, Pallas kernels, attention_far(): pl.pallas_call(far_kernel, out_shape=jax.ShapeDtypeStruct((NSY, NG, ROWS,...  3.34 us
  transfers between devices with their start and end apart: 17, of which 8 were waited for; matrix products, arithmetic and copies ran while one was open for 2% of the time, Pallas kernels for 12%

profile of v3, /device:TPU:1, one launch (start us, length us, event | category | flops | bytes accessed | tf_op | source)
XLA Modules:
  0.0 113.8 jit_solution(18228519963221288994)
XLA Ops:
  0.0 2.3 %kv_send_kernel.1 = bf16[2,8,2,32,256]{4,3,2,1,0:T(8,128)(2,1)} custom-call(s32[1,128]{1,0:T(1,128)} %bitcast.25, bf16[128,1024]{1,0:T(8,128)(2,1)} %k_ref.1, bf16[128,1024]{1,0:T(8,128)(2,1)} %v_ref.1), custom_call_target="tpu_custom_call" | custom-call | tf_op jit(solution)/shard_map/kv_send_kernel/pallas_call | solution.py:277
  2.3 8.6 %all-to-all-start = ((bf16[32,32,256]{2,1,0:T(8,128)(2,1)}), bf16[32,32,256]{2,1,0:T(8,128)(2,1)S(1)}, u32[]{:S(2)}, u32[]{:S(2)}) async-start(bf16[32,32,256]{2,1,0:T(8,128)(2,1)} %bitcast.29), calls=%async_computation | async-start | bytes 1048576 | tf_op jit(solution)/shard_map/all_to_all | solution.py:286
  10.9 0.1 edge_kernel.1.edge_ref
  11.0 7.0 %collective-permute-start = (bf16[16,128]{1,0:T(8,128)(2,1)S(1)}, bf16[16,128]{1,0:T(8,128)(2,1)S(1)}, u32[]{:S(2)}, u32[]{:S(2)}) collective-permute-start(bf16[16,128]{1,0:T(8,128)(2,1)S(1)} %edge_kernel.1.edge_ref), channel_id=1, source_target_pairs={{0,64},{16,80},{32,96},{48,112},{64,0},{80,16},{96,32},{112,48},{1... | collective-permute-start | bytes 12296 | tf_op jit(solution)/shard_map/ppermute | solution.py:290
  18.0 1.6 %q_send_kernel.1 = bf16[2,8,2,32,640]{4,3,2,1,0:T(8,128)(2,1)} custom-call(s32[1,128]{1,0:T(1,128)S(1)} %bitcast.26, bf16[128,5120]{1,0:T(8,128)(2,1)S(1)} %copy-done), custom_call_target="tpu_custom_call" | custom-call | tf_op jit(solution)/shard_map/q_send_kernel/pallas_call | solution.py:277
  19.6 2.1 %all-to-all-done.kv_ref = bf16[32,32,256]{2,1,0:T(8,128)(2,1)S(1)} async-done(((bf16[32,32,256]{2,1,0:T(8,128)(2,1)}), bf16[32,32,256]{2,1,0:T(8,128)(2,1)S(1)}, u32[]{:S(2)}, u32[]{:S(2)}) %all-to-all-start) | async-done | bytes 524320 | tf_op jit(solution)/shard_map/all_to_all | solution.py:286
  21.8 6.0 %all-to-all-start.1 = ((bf16[32,32,640]{2,1,0:T(8,128)(2,1)}), bf16[32,32,640]{2,1,0:T(8,128)(2,1)}, u32[]{:S(2)}, u32[]{:S(2)}) async-start(bf16[32,32,640]{2,1,0:T(8,128)(2,1)} %bitcast.13), calls=%async_computation.1 | async-start | bytes 2621440 | tf_op jit(solution)/shard_map/all_to_all | solution.py:286
  27.7 1.7 %collective-permute-start.1 = (bf16[528,256]{1,0:T(8,128)(2,1)S(1)}, bf16[528,256]{1,0:T(8,128)(2,1)S(1)}, u32[]{:S(2)}, u32[]{:S(2)}) collective-permute-start(bf16[528,256]{1,0:T(8,128)(2,1)S(1)} %get-tuple-element.15.refs_0_), channel_id=1, source_target_pairs={{0,16},{16,32},{32,48},{48,64},{64,80},{80,96},{96,112},{112,0},{1... | collective-permute-start | bytes 811016 | tf_op jit(solution)/shard_map/ppermute | solution.py:290
  29.5 4.0 %collective-permute-start.8 = (bf16[528,256]{1,0:T(8,128)(2,1)S(1)}, bf16[528,256]{1,0:T(8,128)(2,1)S(1)}, u32[]{:S(2)}, u32[]{:S(2)}) collective-permute-start(bf16[528,256]{1,0:T(8,128)(2,1)S(1)} %get-tuple-element.19.refs_0_), channel_id=1, source_target_pairs={{0,112},{16,0},{32,16},{48,32},{64,48},{80,64},{96,80},{112,96},{1... | collective-permute-start | bytes 811016 | tf_op jit(solution)/shard_map/ppermute | solution.py:290
  33.5 1.4 %collective-permute-start.2 = (bf16[528,256]{1,0:T(8,128)(2,1)S(1)}, bf16[528,256]{1,0:T(8,128)(2,1)S(1)}, u32[]{:S(2)}, u32[]{:S(2)}) collective-permute-start(bf16[528,256]{1,0:T(8,128)(2,1)S(1)} %get-tuple-element.15.refs_0_), channel_id=1, source_target_pairs={{0,112},{16,0},{32,16},{48,32},{64,48},{80,64},{96,80},{112,96},{1... | collective-permute-start | bytes 811016 | tf_op jit(solution)/shard_map/ppermute | solution.py:290
  34.9 0.1 collective-permute-start.7
  35.0 5.1 %collective-permute-done.1.refs_1_ = bf16[528,256]{1,0:T(8,128)(2,1)S(1)} collective-permute-done((bf16[528,256]{1,0:T(8,128)(2,1)S(1)}, bf16[528,256]{1,0:T(8,128)(2,1)S(1)}, u32[]{:S(2)}, u32[]{:S(2)}) %collective-permute-start.1) | collective-permute-done | bytes 270368 | tf_op jit(solution)/shard_map/ppermute | solution.py:290
  40.0 0.0 collective-permute-done.8.refs_2_
  40.0 2.7 %collective-permute-start.10 = (bf16[528,256]{1,0:T(8,128)(2,1)S(1)}, bf16[528,256]{1,0:T(8,128)(2,1)S(1)}, u32[]{:S(2)}, u32[]{:S(2)}) collective-permute-start(bf16[528,256]{1,0:T(8,128)(2,1)S(1)} %collective-permute-done.8.refs_2_), channel_id=1, source_target_pairs={{0,112},{16,0},{32,16},{48,32},{64,48},{80,64},{96,80},{112,96},{1... | collective-permute-start | bytes 811016 | tf_op jit(solution)/shard_map/ppermute | solution.py:290
  42.7 2.0 %collective-permute-done.2.refs_2_ = bf16[528,256]{1,0:T(8,128)(2,1)S(1)} collective-permute-done((bf16[528,256]{1,0:T(8,128)(2,1)S(1)}, bf16[528,256]{1,0:T(8,128)(2,1)S(1)}, u32[]{:S(2)}, u32[]{:S(2)}) %collective-permute-start.2) | collective-permute-done | bytes 270368 | tf_op jit(solution)/shard_map/ppermute | solution.py:290
  44.7 3.5 %collective-permute-start.4 = (bf16[528,256]{1,0:T(8,128)(2,1)S(1)}, bf16[528,256]{1,0:T(8,128)(2,1)S(1)}, u32[]{:S(2)}, u32[]{:S(2)}) collective-permute-start(bf16[528,256]{1,0:T(8,128)(2,1)S(1)} %collective-permute-done.2.refs_2_), channel_id=1, source_target_pairs={{0,112},{16,0},{32,16},{48,32},{64,48},{80,64},{96,80},{112,96},{1... | collective-permute-start | bytes 811016 | tf_op jit(solution)/shard_map/ppermute | solution.py:290
  48.3 3.2 %collective-permute-done.3.refs_3_ = bf16[528,256]{1,0:T(8,128)(2,1)S(1)} collective-permute-done((bf16[528,256]{1,0:T(8,128)(2,1)S(1)}, bf16[528,256]{1,0:T(8,128)(2,1)S(1)}, u32[]{:S(2)}, u32[]{:S(2)}) %collective-permute-start.3) | collective-permute-done | bytes 270368 | tf_op jit(solution)/shard_map/ppermute | solution.py:290
  51.5 2.7 %collective-permute-start.12 = (bf16[528,256]{1,0:T(8,128)(2,1)S(1)}, bf16[528,256]{1,0:T(8,128)(2,1)}, u32[]{:S(2)}, u32[]{:S(2)}) collective-permute-start(bf16[528,256]{1,0:T(8,128)(2,1)S(1)} %collective-permute-done.10.refs_4_), channel_id=1, source_target_pairs={{0,112},{16,0},{32,16},{48,32},{64,48},{80,64},{96,80},{112,96},{1... | collective-permute-start | bytes 811016 | tf_op jit(solution)/shard_map/ppermute | solution.py:290
  54.2 0.1 stack.43.info_ref
  54.3 2.1 %collective-permute-done.4.refs_4_ = bf16[528,256]{1,0:T(8,128)(2,1)S(1)} collective-permute-done((bf16[528,256]{1,0:T(8,128)(2,1)S(1)}, bf16[528,256]{1,0:T(8,128)(2,1)S(1)}, u32[]{:S(2)}, u32[]{:S(2)}) %collective-permute-start.4) | collective-permute-done | bytes 270368 | tf_op jit(solution)/shard_map/ppermute | solution.py:290
  56.3 3.4 %collective-permute-start.6 = (bf16[528,256]{1,0:T(8,128)(2,1)S(1)}, bf16[528,256]{1,0:T(8,128)(2,1)}, u32[]{:S(2)}, u32[]{:S(2)}) collective-permute-start(bf16[528,256]{1,0:T(8,128)(2,1)S(1)} %collective-permute-done.4.refs_4_), channel_id=1, source_target_pairs={{0,112},{16,0},{32,16},{48,32},{64,48},{80,64},{96,80},{112,96},{1... | collective-permute-start | bytes 811016 | tf_op jit(solution)/shard_map/ppermute | solution.py:290
  59.7 1.5 %collective-permute-done.5.refs_5_ = bf16[528,256]{1,0:T(8,128)(2,1)} collective-permute-done((bf16[528,256]{1,0:T(8,128)(2,1)S(1)}, bf16[528,256]{1,0:T(8,128)(2,1)}, u32[]{:S(2)}, u32[]{:S(2)}) %collective-permute-start.5) | collective-permute-done | bytes 270368 | tf_op jit(solution)/shard_map/ppermute | solution.py:290
  61.2 0.0 collective-permute-start.13
  61.3 0.9 collective-permute-done.12.refs_6_
  62.1 3.5 %collective-permute-start.14 = (bf16[528,256]{1,0:T(8,128)(2,1)}, bf16[528,256]{1,0:T(8,128)(2,1)S(1)}, u32[]{:S(2)}, u32[]{:S(2)}) collective-permute-start(bf16[528,256]{1,0:T(8,128)(2,1)} %collective-permute-done.12.refs_6_), channel_id=1, source_target_pairs={{0,112},{16,0},{32,16},{48,32},{64,48},{80,64},{96,80},{112,96},{1... | collective-permute-start | bytes 811016 | tf_op jit(solution)/shard_map/ppermute | solution.py:290
  65.6 1.7 %copy_bitcast_fusion.q_ref = bf16[4,5,256,128]{3,2,1,0:T(8,128)(2,1)S(1)} fusion(bf16[32,32,640]{2,1,0:T(8,128)(2,1)} %all-to-all-done.1), kind=kLoop, calls=%fused_computation | loop fusion | bytes 2621440 | tf_op jit(solution)/shard_map/reshape | solution.py:316
  67.3 0.6 collective-permute-done.6.refs_6_
  67.9 6.2 %attention_near.2 = (f32[2,5,256,128]{3,2,1,0:T(8,128)S(1)}, f32[2,5,256,256]{3,2,1,0:T(8,128)S(1)}, s32[4,3]{1,0:T(4,128)S(1)}) custom-call(s32[10]{0:T(128)S(1)} %stack.43.info_ref, s32[1,10]{1,0:T(1,128)S(1)} %bitcast.28, bf16[4,5,256,128]{3,2,1,0:T(8,128)(2,1)S(1)} %copy_bitcast_fusion.q_ref, bf16[528,256]{1,0:T(8,128)(2,1)S(1)} %get-tuple-element.15.refs_0_, ...), custom_call_target="tpu_custom_call" | custom-call | flops 800000000 | bytes 10000000 | tf_op jit(solution)/shard_map/attention_near/pallas_call | solution.py:247
  74.1 5.7 %attention_near.3 = (f32[2,5,256,128]{3,2,1,0:T(8,128)S(1)}, f32[2,5,256,256]{3,2,1,0:T(8,128)S(1)}) custom-call(s32[10]{0:T(128)S(1)} %stack.43.info_ref, s32[4,3]{1,0:T(4,128)S(1)} %get-tuple-element.17.edge_in.edge_ref, bf16[4,5,256,128]{3,2,1,0:T(8,128)(2,1)S(1)} %copy_bitcast_fusion.q_ref, bf16[528,256]{1,0:T(8,128)(2,1)S(1)} %get-tuple-element.19.refs_0_, ...), custom_call_target="tpu_custom_call" | custom-call | flops 800000000 | bytes 10000000 | tf_op jit(solution)/shard_map/attention_near/pallas_call | solution.py:247
  79.9 3.3 %attention_far.1 = bf16[32,4,8,640]{3,2,1,0:T(8,128)(2,1)S(1)} custom-call(s32[10]{0:T(128)S(1)} %stack.43.info_ref, s32[4,3]{1,0:T(4,128)S(1)} %get-tuple-element.17.edge_in.edge_ref, bf16[4,5,256,128]{3,2,1,0:T(8,128)(2,1)S(1)} %copy_bitcast_fusion.q_ref, f32[2,5,256,128]{3,2,1,0:T(8,128)S(1)} %get-tuple-element.18.refs_0_, ...), custom_call_target="tpu_custom_call" | custom-call | flops 800000000 | bytes 7000000 | tf_op jit(solution)/shard_map/attention_far/pallas_call | solution.py:263
  83.2 29.1 %all_to_all.15 = bf16[32,32,640]{2,1,0:T(8,128)(2,1)S(1)} all-to-all(bf16[32,32,640]{2,1,0:T(8,128)(2,1)S(1)} %bitcast.23), channel_id=1, replica_groups=mesh['yl'=2,'z'=8,'yh'=2,'x'=4,'c'=2] {'yh','x','c','yl'}, dimensions={0} | all-to-all | bytes 2621440 | tf_op jit(solution)/shard_map/all_to_all | solution.py:286
  112.3 1.3 %put_back.1 = bf16[128,5120]{1,0:T(8,128)(2,1)} custom-call(s32[1,128]{1,0:T(1,128)S(1)} %bitcast.27, bf16[2,8,2,32,640]{4,3,2,1,0:T(8,128)(2,1)S(1)} %bitcast.24), custom_call_target="tpu_custom_call" | custom-call | tf_op jit(solution)/shard_map/put_back/pallas_call | solution.py:328
  (19 shorter events, 0.1 us)
Async XLA Ops:
  0.0 18.0 %copy-start.2 = (s32[1,1,128]{2,1,0:T(1,128)S(1)}, s32[1,1,128]{2,1,0:T(1,128)}, u32[]{:S(2)}) copy-start(s32[1,1,128]{2,1,0:T(1,128)} %param.8) | copy-start | bytes 1540
  0.0 10.9 %copy-start.1 = (s32[1,2048]{1,0:T(1,128)S(1)}, s32[1,2048]{1,0:T(1,128)}, u32[]{:S(2)}) copy-start(s32[1,2048]{1,0:T(1,128)} %doc_ref) | copy-start | bytes 24580
  0.0 18.0 %copy-start = (bf16[128,5120]{1,0:T(8,128)(2,1)S(1)}, bf16[128,5120]{1,0:T(8,128)(2,1)}, u32[]{:S(2)}) copy-start(bf16[128,5120]{1,0:T(8,128)(2,1)} %q_ref.1) | copy-start | bytes 3932164
  2.3 19.4 %all-to-all-start = ((bf16[32,32,256]{2,1,0:T(8,128)(2,1)}), bf16[32,32,256]{2,1,0:T(8,128)(2,1)S(1)}, u32[]{:S(2)}, u32[]{:S(2)}) async-start(bf16[32,32,256]{2,1,0:T(8,128)(2,1)} %bitcast.29), calls=%async_computation | async-start | bytes 1048576 | tf_op jit(solution)/shard_map/all_to_all | solution.py:286
  11.0 8.6 %collective-permute-start = (bf16[16,128]{1,0:T(8,128)(2,1)S(1)}, bf16[16,128]{1,0:T(8,128)(2,1)S(1)}, u32[]{:S(2)}, u32[]{:S(2)}) collective-permute-start(bf16[16,128]{1,0:T(8,128)(2,1)S(1)} %edge_kernel.1.edge_ref), channel_id=1, source_target_pairs={{0,64},{16,80},{32,96},{48,112},{64,0},{80,16},{96,32},{112,48},{1... | collective-permute-start | bytes 12296 | tf_op jit(solution)/shard_map/ppermute | solution.py:290
  21.8 43.9 %all-to-all-start.1 = ((bf16[32,32,640]{2,1,0:T(8,128)(2,1)}), bf16[32,32,640]{2,1,0:T(8,128)(2,1)}, u32[]{:S(2)}, u32[]{:S(2)}) async-start(bf16[32,32,640]{2,1,0:T(8,128)(2,1)} %bitcast.13), calls=%async_computation.1 | async-start | bytes 2621440 | tf_op jit(solution)/shard_map/all_to_all | solution.py:286
  27.7 12.3 %collective-permute-start.1 = (bf16[528,256]{1,0:T(8,128)(2,1)S(1)}, bf16[528,256]{1,0:T(8,128)(2,1)S(1)}, u32[]{:S(2)}, u32[]{:S(2)}) collective-permute-start(bf16[528,256]{1,0:T(8,128)(2,1)S(1)} %get-tuple-element.15.refs_0_), channel_id=1, source_target_pairs={{0,16},{16,32},{32,48},{48,64},{64,80},{80,96},{96,112},{112,0},{1... | collective-permute-start | bytes 811016 | tf_op jit(solution)/shard_map/ppermute | solution.py:290
  29.5 10.6 %collective-permute-start.8 = (bf16[528,256]{1,0:T(8,128)(2,1)S(1)}, bf16[528,256]{1,0:T(8,128)(2,1)S(1)}, u32[]{:S(2)}, u32[]{:S(2)}) collective-permute-start(bf16[528,256]{1,0:T(8,128)(2,1)S(1)} %get-tuple-element.19.refs_0_), channel_id=1, source_target_pairs={{0,112},{16,0},{32,16},{48,32},{64,48},{80,64},{96,80},{112,96},{1... | collective-permute-start | bytes 811016 | tf_op jit(solution)/shard_map/ppermute | solution.py:290
  33.5 11.2 %collective-permute-start.2 = (bf16[528,256]{1,0:T(8,128)(2,1)S(1)}, bf16[528,256]{1,0:T(8,128)(2,1)S(1)}, u32[]{:S(2)}, u32[]{:S(2)}) collective-permute-start(bf16[528,256]{1,0:T(8,128)(2,1)S(1)} %get-tuple-element.15.refs_0_), channel_id=1, source_target_pairs={{0,112},{16,0},{32,16},{48,32},{64,48},{80,64},{96,80},{112,96},{1... | collective-permute-start | bytes 811016 | tf_op jit(solution)/shard_map/ppermute | solution.py:290
  34.9 13.4 %collective-permute-start.7 = (bf16[528,256]{1,0:T(8,128)(2,1)S(1)}, bf16[528,256]{1,0:T(8,128)(2,1)S(1)}, u32[]{:S(2)}, u32[]{:S(2)}) collective-permute-start(bf16[528,256]{1,0:T(8,128)(2,1)S(1)} %get-tuple-element.19.refs_0_), channel_id=1, source_target_pairs={{0,16},{16,32},{32,48},{48,64},{64,80},{80,96},{96,112},{112,0},{1... | collective-permute-start | bytes 811016 | tf_op jit(solution)/shard_map/ppermute | solution.py:290
  40.0 11.5 %collective-permute-start.3 = (bf16[528,256]{1,0:T(8,128)(2,1)S(1)}, bf16[528,256]{1,0:T(8,128)(2,1)S(1)}, u32[]{:S(2)}, u32[]{:S(2)}) collective-permute-start(bf16[528,256]{1,0:T(8,128)(2,1)S(1)} %collective-permute-done.1.refs_1_), channel_id=1, source_target_pairs={{0,16},{16,32},{32,48},{48,64},{64,80},{80,96},{96,112},{112,0},{1... | collective-permute-start | bytes 811016 | tf_op jit(solution)/shard_map/ppermute | solution.py:290
  40.0 11.5 %collective-permute-start.10 = (bf16[528,256]{1,0:T(8,128)(2,1)S(1)}, bf16[528,256]{1,0:T(8,128)(2,1)S(1)}, u32[]{:S(2)}, u32[]{:S(2)}) collective-permute-start(bf16[528,256]{1,0:T(8,128)(2,1)S(1)} %collective-permute-done.8.refs_2_), channel_id=1, source_target_pairs={{0,112},{16,0},{32,16},{48,32},{64,48},{80,64},{96,80},{112,96},{1... | collective-permute-start | bytes 811016 | tf_op jit(solution)/shard_map/ppermute | solution.py:290
  44.7 11.6 %collective-permute-start.4 = (bf16[528,256]{1,0:T(8,128)(2,1)S(1)}, bf16[528,256]{1,0:T(8,128)(2,1)S(1)}, u32[]{:S(2)}, u32[]{:S(2)}) collective-permute-start(bf16[528,256]{1,0:T(8,128)(2,1)S(1)} %collective-permute-done.2.refs_2_), channel_id=1, source_target_pairs={{0,112},{16,0},{32,16},{48,32},{64,48},{80,64},{96,80},{112,96},{1... | collective-permute-start | bytes 811016 | tf_op jit(solution)/shard_map/ppermute | solution.py:290
  48.3 11.5 %collective-permute-start.9 = (bf16[528,256]{1,0:T(8,128)(2,1)S(1)}, bf16[528,256]{1,0:T(8,128)(2,1)S(1)}, u32[]{:S(2)}, u32[]{:S(2)}) collective-permute-start(bf16[528,256]{1,0:T(8,128)(2,1)S(1)} %collective-permute-done.7.refs_1_), channel_id=1, source_target_pairs={{0,16},{16,32},{32,48},{48,64},{64,80},{80,96},{96,112},{112,0},{1... | collective-permute-start | bytes 811016 | tf_op jit(solution)/shard_map/ppermute | solution.py:290
  51.5 9.7 %collective-permute-start.5 = (bf16[528,256]{1,0:T(8,128)(2,1)S(1)}, bf16[528,256]{1,0:T(8,128)(2,1)}, u32[]{:S(2)}, u32[]{:S(2)}) collective-permute-start(bf16[528,256]{1,0:T(8,128)(2,1)S(1)} %collective-permute-done.3.refs_3_), channel_id=1, source_target_pairs={{0,16},{16,32},{32,48},{48,64},{64,80},{80,96},{96,112},{112,0},{1... | collective-permute-start | bytes 811016 | tf_op jit(solution)/shard_map/ppermute | solution.py:290
  51.5 10.6 %collective-permute-start.12 = (bf16[528,256]{1,0:T(8,128)(2,1)S(1)}, bf16[528,256]{1,0:T(8,128)(2,1)}, u32[]{:S(2)}, u32[]{:S(2)}) collective-permute-start(bf16[528,256]{1,0:T(8,128)(2,1)S(1)} %collective-permute-done.10.refs_4_), channel_id=1, source_target_pairs={{0,112},{16,0},{32,16},{48,32},{64,48},{80,64},{96,80},{112,96},{1... | collective-permute-start | bytes 811016 | tf_op jit(solution)/shard_map/ppermute | solution.py:290
  56.3 11.6 %collective-permute-start.6 = (bf16[528,256]{1,0:T(8,128)(2,1)S(1)}, bf16[528,256]{1,0:T(8,128)(2,1)}, u32[]{:S(2)}, u32[]{:S(2)}) collective-permute-start(bf16[528,256]{1,0:T(8,128)(2,1)S(1)} %collective-permute-done.4.refs_4_), channel_id=1, source_target_pairs={{0,112},{16,0},{32,16},{48,32},{64,48},{80,64},{96,80},{112,96},{1... | collective-permute-start | bytes 811016 | tf_op jit(solution)/shard_map/ppermute | solution.py:290
  59.7 14.4 %collective-permute-start.11 = (bf16[528,256]{1,0:T(8,128)(2,1)S(1)}, bf16[528,256]{1,0:T(8,128)(2,1)}, u32[]{:S(2)}, u32[]{:S(2)}) collective-permute-start(bf16[528,256]{1,0:T(8,128)(2,1)S(1)} %collective-permute-done.9.refs_3_), channel_id=1, source_target_pairs={{0,16},{16,32},{32,48},{48,64},{64,80},{80,96},{96,112},{112,0},{1... | collective-permute-start | bytes 811016 | tf_op jit(solution)/shard_map/ppermute | solution.py:290
  61.2 18.6 %collective-permute-start.13 = (bf16[528,256]{1,0:T(8,128)(2,1)}, bf16[528,256]{1,0:T(8,128)(2,1)S(1)}, u32[]{:S(2)}, u32[]{:S(2)}) collective-permute-start(bf16[528,256]{1,0:T(8,128)(2,1)} %collective-permute-done.5.refs_5_), channel_id=1, source_target_pairs={{0,16},{16,32},{32,48},{48,64},{64,80},{80,96},{96,112},{112,0},{1... | collective-permute-start | bytes 811016 | tf_op jit(solution)/shard_map/ppermute | solution.py:290
  62.1 17.7 %collective-permute-start.14 = (bf16[528,256]{1,0:T(8,128)(2,1)}, bf16[528,256]{1,0:T(8,128)(2,1)S(1)}, u32[]{:S(2)}, u32[]{:S(2)}) collective-permute-start(bf16[528,256]{1,0:T(8,128)(2,1)} %collective-permute-done.12.refs_6_), channel_id=1, source_target_pairs={{0,112},{16,0},{32,16},{48,32},{64,48},{80,64},{96,80},{112,96},{1... | collective-permute-start | bytes 811016 | tf_op jit(solution)/shard_map/ppermute | solution.py:290

commit v4 on v3

--- a/solution.py
+++ b/solution.py
@@ -44,10 +44,16 @@
     ).astype(jnp.bfloat16)
 
 
-def kv_send_kernel(slot_ref, k_ref, v_ref, o_ref):
+def kv_send_kernel(slot_ref, k_ref, v_ref, o_ref, buf, sems):
+    loads = [
+        pltpu.make_async_copy(ref, buf.at[i], sems.at[i]) for i, ref in enumerate((k_ref, v_ref))
+    ]
+    for load in loads:
+        load.start()
     onehot = one_hot_t(slot_ref[...])
-    for part, ref in enumerate((k_ref, v_ref)):
-        got = pick(onehot, ref[...])
+    for part in range(2):
+        loads[part].wait()
+        got = pick(onehot, buf[part])
         for h in range(KVH):
             for yl in range(2):
                 for yh in range(2):
@@ -295,9 +301,19 @@
     bf16 = jnp.bfloat16
     z0 = lax.axis_index("z")
 
-    kv_out = whole(
-        kv_send_kernel, 60, jax.ShapeDtypeStruct((2, KVH, 2, 32, 2 * HD), bf16), slot, keys, values
-    )
+    vmem, anywhere = pl.BlockSpec(memory_space=pltpu.VMEM), pl.BlockSpec(memory_space=pl.ANY)
+    kv_out = pl.pallas_call(
+        kv_send_kernel,
+        out_shape=jax.ShapeDtypeStruct((2, KVH, 2, 32, 2 * HD), bf16),
+        in_specs=[vmem, anywhere, anywhere],
+        out_specs=vmem,
+        scratch_shapes=[
+            pltpu.VMEM((2, 128, KVH * HD), bf16),
+            pltpu.SemaphoreType.DMA((2,)),
+        ],
+        compiler_params=pltpu.CompilerParams(vmem_limit_bytes=60 * 1024 * 1024),
+        name="kv_send_kernel",
+    )(slot, keys, values)
     q_out = whole(q_send_kernel, 24, jax.ShapeDtypeStruct((2, KVH, 2, 32, GS * HD), bf16), slot, queries)
     kv = swap(kv_out.reshape(NSY, 32, 2 * HD), PLANE)
     _, doc_ids = lax.optimization_barrier((kv_out, doc_ids))

time: 114 us -> 115 us (level); the launches traced: 114 us -> 113 us
    pallas_call x0 -> x1, Pallas kernels: none -> 3 us  [on_device(): pl.pallas_call(kv_send_kernel, out_shape=jax.ShapeDtypeStruct((2, KVH, 2,...]
    pallas_call x4 -> x3, Pallas kernels: 4.03 us -> 1.76 us  [whole(): pl.pallas_call(kernel, out_shape=out_shape, compiler_params=pltpu.Compile...]
  transfers between devices with their start and end apart: 17 -> 17, of which waited for: 8 -> 8; matrix products, arithmetic and copies ran while one was open for 2% -> 2% of each run, Pallas kernels for 12% -> 11%
where the time goes in v4:
time: 115 us; the launch traced here: 113 us
  starting transfers between devices  44.6 us (39%)
  blocking collectives  28.9 us (25%)
  Pallas kernels  20.4 us (18%)
  waiting for transfers between devices  17.5 us (15%)
  local copies, waits for them, and re-layouts  1.75 us (2%)
    ppermute x15, starting transfers between devices, along_z(): return lax.ppermute(value, 'z', [(i, (i + step) % NZ) for i in range(NZ)])  30 us
    all_to_all x1, blocking collectives, swap(): return lax.all_to_all(value, axes, split_axis=0, concat_axis=0, tiled=True)  28.9 us
    ppermute x15, waiting for transfers between devices, along_z(): return lax.ppermute(value, 'z', [(i, (i + step) % NZ) for i in range(NZ)])  15.4 us
    all_to_all x2, starting transfers between devices, swap(): return lax.all_to_all(value, axes, split_axis=0, concat_axis=0, tiled=True)  14.6 us
    pallas_call x2, Pallas kernels, attention_near(): pl.pallas_call(functools.partial(near_kernel, chunk), out_shape=out_shape...  10.9 us
    pallas_call x1, Pallas kernels, attention_far(): pl.pallas_call(far_kernel, out_shape=jax.ShapeDtypeStruct((NSY, NG, ROWS,...  3.34 us
    pallas_call x1, Pallas kernels, on_device(): pl.pallas_call(kv_send_kernel, out_shape=jax.ShapeDtypeStruct((2, KVH, 2,...  3 us
  transfers between devices with their start and end apart: 17, of which 8 were waited for; matrix products, arithmetic and copies ran while one was open for 2% of the time, Pallas kernels for 11%

profile of v4, /device:TPU:1, one launch (start us, length us, event | category | flops | bytes accessed | tf_op | source)
XLA Modules:
  0.0 113.4 jit_solution(3646141806078089585)
XLA Ops:
  0.0 3.0 %kv_send_kernel.1 = bf16[2,8,2,32,256]{4,3,2,1,0:T(8,128)(2,1)} custom-call(s32[1,128]{1,0:T(1,128)} %bitcast.25, bf16[128,1024]{1,0:T(8,128)(2,1)} %k_ref.1, bf16[128,1024]{1,0:T(8,128)(2,1)} %v_ref.1), custom_call_target="tpu_custom_call" | custom-call | tf_op jit(solution)/shard_map/kv_send_kernel/pallas_call | solution.py:305
  3.0 8.6 %all-to-all-start = ((bf16[32,32,256]{2,1,0:T(8,128)(2,1)}), bf16[32,32,256]{2,1,0:T(8,128)(2,1)S(1)}, u32[]{:S(2)}, u32[]{:S(2)}) async-start(bf16[32,32,256]{2,1,0:T(8,128)(2,1)} %bitcast.29), calls=%async_computation | async-start | bytes 1048576 | tf_op jit(solution)/shard_map/all_to_all | solution.py:292
  11.6 0.1 edge_kernel.1.edge_ref
  11.8 7.0 %collective-permute-start = (bf16[16,128]{1,0:T(8,128)(2,1)S(1)}, bf16[16,128]{1,0:T(8,128)(2,1)S(1)}, u32[]{:S(2)}, u32[]{:S(2)}) collective-permute-start(bf16[16,128]{1,0:T(8,128)(2,1)S(1)} %edge_kernel.1.edge_ref), channel_id=1, source_target_pairs={{0,64},{16,80},{32,96},{48,112},{64,0},{80,16},{96,32},{112,48},{1... | collective-permute-start | bytes 12296 | tf_op jit(solution)/shard_map/ppermute | solution.py:296
  18.8 1.6 %q_send_kernel.1 = bf16[2,8,2,32,640]{4,3,2,1,0:T(8,128)(2,1)} custom-call(s32[1,128]{1,0:T(1,128)S(1)} %bitcast.26, bf16[128,5120]{1,0:T(8,128)(2,1)S(1)} %copy-done), custom_call_target="tpu_custom_call" | custom-call | tf_op jit(solution)/shard_map/q_send_kernel/pallas_call | solution.py:283
  20.4 0.0 collective-permute-done.far_ref
  20.4 2.1 %all-to-all-done.kv_ref = bf16[32,32,256]{2,1,0:T(8,128)(2,1)S(1)} async-done(((bf16[32,32,256]{2,1,0:T(8,128)(2,1)}), bf16[32,32,256]{2,1,0:T(8,128)(2,1)S(1)}, u32[]{:S(2)}, u32[]{:S(2)}) %all-to-all-start) | async-done | bytes 524320 | tf_op jit(solution)/shard_map/all_to_all | solution.py:292
  22.5 6.0 %all-to-all-start.1 = ((bf16[32,32,640]{2,1,0:T(8,128)(2,1)}), bf16[32,32,640]{2,1,0:T(8,128)(2,1)}, u32[]{:S(2)}, u32[]{:S(2)}) async-start(bf16[32,32,640]{2,1,0:T(8,128)(2,1)} %bitcast.13), calls=%async_computation.1 | async-start | bytes 2621440 | tf_op jit(solution)/shard_map/all_to_all | solution.py:292
  28.5 1.7 %collective-permute-start.1 = (bf16[528,256]{1,0:T(8,128)(2,1)S(1)}, bf16[528,256]{1,0:T(8,128)(2,1)S(1)}, u32[]{:S(2)}, u32[]{:S(2)}) collective-permute-start(bf16[528,256]{1,0:T(8,128)(2,1)S(1)} %get-tuple-element.15.refs_0_), channel_id=1, source_target_pairs={{0,16},{16,32},{32,48},{48,64},{64,80},{80,96},{96,112},{112,0},{1... | collective-permute-start | bytes 811016 | tf_op jit(solution)/shard_map/ppermute | solution.py:296
  30.2 4.0 %collective-permute-start.8 = (bf16[528,256]{1,0:T(8,128)(2,1)S(1)}, bf16[528,256]{1,0:T(8,128)(2,1)S(1)}, u32[]{:S(2)}, u32[]{:S(2)}) collective-permute-start(bf16[528,256]{1,0:T(8,128)(2,1)S(1)} %get-tuple-element.19.refs_0_), channel_id=1, source_target_pairs={{0,112},{16,0},{32,16},{48,32},{64,48},{80,64},{96,80},{112,96},{1... | collective-permute-start | bytes 811016 | tf_op jit(solution)/shard_map/ppermute | solution.py:296
  34.2 1.4 %collective-permute-start.2 = (bf16[528,256]{1,0:T(8,128)(2,1)S(1)}, bf16[528,256]{1,0:T(8,128)(2,1)S(1)}, u32[]{:S(2)}, u32[]{:S(2)}) collective-permute-start(bf16[528,256]{1,0:T(8,128)(2,1)S(1)} %get-tuple-element.15.refs_0_), channel_id=1, source_target_pairs={{0,112},{16,0},{32,16},{48,32},{64,48},{80,64},{96,80},{112,96},{1... | collective-permute-start | bytes 811016 | tf_op jit(solution)/shard_map/ppermute | solution.py:296
  35.6 0.1 collective-permute-start.7
  35.7 5.1 %collective-permute-done.1.refs_1_ = bf16[528,256]{1,0:T(8,128)(2,1)S(1)} collective-permute-done((bf16[528,256]{1,0:T(8,128)(2,1)S(1)}, bf16[528,256]{1,0:T(8,128)(2,1)S(1)}, u32[]{:S(2)}, u32[]{:S(2)}) %collective-permute-start.1) | collective-permute-done | bytes 270368 | tf_op jit(solution)/shard_map/ppermute | solution.py:296
  40.8 2.7 %collective-permute-start.10 = (bf16[528,256]{1,0:T(8,128)(2,1)S(1)}, bf16[528,256]{1,0:T(8,128)(2,1)S(1)}, u32[]{:S(2)}, u32[]{:S(2)}) collective-permute-start(bf16[528,256]{1,0:T(8,128)(2,1)S(1)} %collective-permute-done.8.refs_2_), channel_id=1, source_target_pairs={{0,112},{16,0},{32,16},{48,32},{64,48},{80,64},{96,80},{112,96},{1... | collective-permute-start | bytes 811016 | tf_op jit(solution)/shard_map/ppermute | solution.py:296
  43.4 2.0 %collective-permute-done.2.refs_2_ = bf16[528,256]{1,0:T(8,128)(2,1)S(1)} collective-permute-done((bf16[528,256]{1,0:T(8,128)(2,1)S(1)}, bf16[528,256]{1,0:T(8,128)(2,1)S(1)}, u32[]{:S(2)}, u32[]{:S(2)}) %collective-permute-start.2) | collective-permute-done | bytes 270368 | tf_op jit(solution)/shard_map/ppermute | solution.py:296
  45.5 3.5 %collective-permute-start.4 = (bf16[528,256]{1,0:T(8,128)(2,1)S(1)}, bf16[528,256]{1,0:T(8,128)(2,1)S(1)}, u32[]{:S(2)}, u32[]{:S(2)}) collective-permute-start(bf16[528,256]{1,0:T(8,128)(2,1)S(1)} %collective-permute-done.2.refs_2_), channel_id=1, source_target_pairs={{0,112},{16,0},{32,16},{48,32},{64,48},{80,64},{96,80},{112,96},{1... | collective-permute-start | bytes 811016 | tf_op jit(solution)/shard_map/ppermute | solution.py:296
  49.0 3.2 %collective-permute-done.3.refs_3_ = bf16[528,256]{1,0:T(8,128)(2,1)S(1)} collective-permute-done((bf16[528,256]{1,0:T(8,128)(2,1)S(1)}, bf16[528,256]{1,0:T(8,128)(2,1)S(1)}, u32[]{:S(2)}, u32[]{:S(2)}) %collective-permute-start.3) | collective-permute-done | bytes 270368 | tf_op jit(solution)/shard_map/ppermute | solution.py:296
  52.2 2.7 %collective-permute-start.12 = (bf16[528,256]{1,0:T(8,128)(2,1)S(1)}, bf16[528,256]{1,0:T(8,128)(2,1)}, u32[]{:S(2)}, u32[]{:S(2)}) collective-permute-start(bf16[528,256]{1,0:T(8,128)(2,1)S(1)} %collective-permute-done.10.refs_4_), channel_id=1, source_target_pairs={{0,112},{16,0},{32,16},{48,32},{64,48},{80,64},{96,80},{112,96},{1... | collective-permute-start | bytes 811016 | tf_op jit(solution)/shard_map/ppermute | solution.py:296
  54.9 0.1 stack.43.info_ref
  55.0 2.1 %collective-permute-done.4.refs_4_ = bf16[528,256]{1,0:T(8,128)(2,1)S(1)} collective-permute-done((bf16[528,256]{1,0:T(8,128)(2,1)S(1)}, bf16[528,256]{1,0:T(8,128)(2,1)S(1)}, u32[]{:S(2)}, u32[]{:S(2)}) %collective-permute-start.4) | collective-permute-done | bytes 270368 | tf_op jit(solution)/shard_map/ppermute | solution.py:296
  57.1 3.4 %collective-permute-start.6 = (bf16[528,256]{1,0:T(8,128)(2,1)S(1)}, bf16[528,256]{1,0:T(8,128)(2,1)}, u32[]{:S(2)}, u32[]{:S(2)}) collective-permute-start(bf16[528,256]{1,0:T(8,128)(2,1)S(1)} %collective-permute-done.4.refs_4_), channel_id=1, source_target_pairs={{0,112},{16,0},{32,16},{48,32},{64,48},{80,64},{96,80},{112,96},{1... | collective-permute-start | bytes 811016 | tf_op jit(solution)/shard_map/ppermute | solution.py:296
  60.5 1.5 %collective-permute-done.5.refs_5_ = bf16[528,256]{1,0:T(8,128)(2,1)} collective-permute-done((bf16[528,256]{1,0:T(8,128)(2,1)S(1)}, bf16[528,256]{1,0:T(8,128)(2,1)}, u32[]{:S(2)}, u32[]{:S(2)}) %collective-permute-start.5) | collective-permute-done | bytes 270368 | tf_op jit(solution)/shard_map/ppermute | solution.py:296
  62.0 0.0 collective-permute-start.13
  62.0 0.9 collective-permute-done.12.refs_6_
  62.9 3.5 %collective-permute-start.14 = (bf16[528,256]{1,0:T(8,128)(2,1)}, bf16[528,256]{1,0:T(8,128)(2,1)S(1)}, u32[]{:S(2)}, u32[]{:S(2)}) collective-permute-start(bf16[528,256]{1,0:T(8,128)(2,1)} %collective-permute-done.12.refs_6_), channel_id=1, source_target_pairs={{0,112},{16,0},{32,16},{48,32},{64,48},{80,64},{96,80},{112,96},{1... | collective-permute-start | bytes 811016 | tf_op jit(solution)/shard_map/ppermute | solution.py:296
  66.4 1.7 %copy_bitcast_fusion.q_ref = bf16[4,5,256,128]{3,2,1,0:T(8,128)(2,1)S(1)} fusion(bf16[32,32,640]{2,1,0:T(8,128)(2,1)} %all-to-all-done.1), kind=kLoop, calls=%fused_computation | loop fusion | bytes 2621440 | tf_op jit(solution)/shard_map/reshape | solution.py:332
  68.0 0.6 collective-permute-done.6.refs_6_
  68.7 5.7 %attention_near.2 = (f32[2,5,256,128]{3,2,1,0:T(8,128)S(1)}, f32[2,5,256,256]{3,2,1,0:T(8,128)S(1)}, s32[4,3]{1,0:T(4,128)S(1)}) custom-call(s32[10]{0:T(128)S(1)} %stack.43.info_ref, s32[1,10]{1,0:T(1,128)S(1)} %bitcast.28, bf16[4,5,256,128]{3,2,1,0:T(8,128)(2,1)S(1)} %copy_bitcast_fusion.q_ref, bf16[528,256]{1,0:T(8,128)(2,1)S(1)} %get-tuple-element.15.refs_0_, ...), custom_call_target="tpu_custom_call" | custom-call | flops 800000000 | bytes 10000000 | tf_op jit(solution)/shard_map/attention_near/pallas_call | solution.py:253
  74.4 5.2 %attention_near.3 = (f32[2,5,256,128]{3,2,1,0:T(8,128)S(1)}, f32[2,5,256,256]{3,2,1,0:T(8,128)S(1)}) custom-call(s32[10]{0:T(128)S(1)} %stack.43.info_ref, s32[4,3]{1,0:T(4,128)S(1)} %get-tuple-element.17.edge_in.edge_ref, bf16[4,5,256,128]{3,2,1,0:T(8,128)(2,1)S(1)} %copy_bitcast_fusion.q_ref, bf16[528,256]{1,0:T(8,128)(2,1)S(1)} %get-tuple-element.19.refs_0_, ...), custom_call_target="tpu_custom_call" | custom-call | flops 800000000 | bytes 10000000 | tf_op jit(solution)/shard_map/attention_near/pallas_call | solution.py:253
  79.6 3.3 %attention_far.1 = bf16[32,4,8,640]{3,2,1,0:T(8,128)(2,1)S(1)} custom-call(s32[10]{0:T(128)S(1)} %stack.43.info_ref, s32[4,3]{1,0:T(4,128)S(1)} %get-tuple-element.17.edge_in.edge_ref, bf16[4,5,256,128]{3,2,1,0:T(8,128)(2,1)S(1)} %copy_bitcast_fusion.q_ref, f32[2,5,256,128]{3,2,1,0:T(8,128)S(1)} %get-tuple-element.18.refs_0_, ...), custom_call_target="tpu_custom_call" | custom-call | flops 800000000 | bytes 7000000 | tf_op jit(solution)/shard_map/attention_far/pallas_call | solution.py:269
  83.0 28.9 %all_to_all.15 = bf16[32,32,640]{2,1,0:T(8,128)(2,1)S(1)} all-to-all(bf16[32,32,640]{2,1,0:T(8,128)(2,1)S(1)} %bitcast.23), channel_id=1, replica_groups=mesh['yl'=2,'z'=8,'yh'=2,'x'=4,'c'=2] {'yh','x','c','yl'}, dimensions={0} | all-to-all | bytes 2621440 | tf_op jit(solution)/shard_map/all_to_all | solution.py:292
  111.9 1.3 %put_back.1 = bf16[128,5120]{1,0:T(8,128)(2,1)} custom-call(s32[1,128]{1,0:T(1,128)S(1)} %bitcast.27, bf16[2,8,2,32,640]{4,3,2,1,0:T(8,128)(2,1)S(1)} %bitcast.24), custom_call_target="tpu_custom_call" | custom-call | tf_op jit(solution)/shard_map/put_back/pallas_call | solution.py:344
  (19 shorter events, 0.1 us)
Async XLA Ops:
  0.0 18.8 %copy-start.2 = (s32[1,1,128]{2,1,0:T(1,128)S(1)}, s32[1,1,128]{2,1,0:T(1,128)}, u32[]{:S(2)}) copy-start(s32[1,1,128]{2,1,0:T(1,128)} %param.8) | copy-start | bytes 1540
  0.0 11.6 %copy-start.1 = (s32[1,2048]{1,0:T(1,128)S(1)}, s32[1,2048]{1,0:T(1,128)}, u32[]{:S(2)}) copy-start(s32[1,2048]{1,0:T(1,128)} %doc_ref) | copy-start | bytes 24580
  0.0 18.8 %copy-start = (bf16[128,5120]{1,0:T(8,128)(2,1)S(1)}, bf16[128,5120]{1,0:T(8,128)(2,1)}, u32[]{:S(2)}) copy-start(bf16[128,5120]{1,0:T(8,128)(2,1)} %q_ref.1) | copy-start | bytes 3932164
  3.0 19.4 %all-to-all-start = ((bf16[32,32,256]{2,1,0:T(8,128)(2,1)}), bf16[32,32,256]{2,1,0:T(8,128)(2,1)S(1)}, u32[]{:S(2)}, u32[]{:S(2)}) async-start(bf16[32,32,256]{2,1,0:T(8,128)(2,1)} %bitcast.29), calls=%async_computation | async-start | bytes 1048576 | tf_op jit(solution)/shard_map/all_to_all | solution.py:292
  11.8 8.6 %collective-permute-start = (bf16[16,128]{1,0:T(8,128)(2,1)S(1)}, bf16[16,128]{1,0:T(8,128)(2,1)S(1)}, u32[]{:S(2)}, u32[]{:S(2)}) collective-permute-start(bf16[16,128]{1,0:T(8,128)(2,1)S(1)} %edge_kernel.1.edge_ref), channel_id=1, source_target_pairs={{0,64},{16,80},{32,96},{48,112},{64,0},{80,16},{96,32},{112,48},{1... | collective-permute-start | bytes 12296 | tf_op jit(solution)/shard_map/ppermute | solution.py:296
  22.5 43.9 %all-to-all-start.1 = ((bf16[32,32,640]{2,1,0:T(8,128)(2,1)}), bf16[32,32,640]{2,1,0:T(8,128)(2,1)}, u32[]{:S(2)}, u32[]{:S(2)}) async-start(bf16[32,32,640]{2,1,0:T(8,128)(2,1)} %bitcast.13), calls=%async_computation.1 | async-start | bytes 2621440 | tf_op jit(solution)/shard_map/all_to_all | solution.py:292
  28.5 12.3 %collective-permute-start.1 = (bf16[528,256]{1,0:T(8,128)(2,1)S(1)}, bf16[528,256]{1,0:T(8,128)(2,1)S(1)}, u32[]{:S(2)}, u32[]{:S(2)}) collective-permute-start(bf16[528,256]{1,0:T(8,128)(2,1)S(1)} %get-tuple-element.15.refs_0_), channel_id=1, source_target_pairs={{0,16},{16,32},{32,48},{48,64},{64,80},{80,96},{96,112},{112,0},{1... | collective-permute-start | bytes 811016 | tf_op jit(solution)/shard_map/ppermute | solution.py:296
  30.2 10.6 %collective-permute-start.8 = (bf16[528,256]{1,0:T(8,128)(2,1)S(1)}, bf16[528,256]{1,0:T(8,128)(2,1)S(1)}, u32[]{:S(2)}, u32[]{:S(2)}) collective-permute-start(bf16[528,256]{1,0:T(8,128)(2,1)S(1)} %get-tuple-element.19.refs_0_), channel_id=1, source_target_pairs={{0,112},{16,0},{32,16},{48,32},{64,48},{80,64},{96,80},{112,96},{1... | collective-permute-start | bytes 811016 | tf_op jit(solution)/shard_map/ppermute | solution.py:296
  34.2 11.2 %collective-permute-start.2 = (bf16[528,256]{1,0:T(8,128)(2,1)S(1)}, bf16[528,256]{1,0:T(8,128)(2,1)S(1)}, u32[]{:S(2)}, u32[]{:S(2)}) collective-permute-start(bf16[528,256]{1,0:T(8,128)(2,1)S(1)} %get-tuple-element.15.refs_0_), channel_id=1, source_target_pairs={{0,112},{16,0},{32,16},{48,32},{64,48},{80,64},{96,80},{112,96},{1... | collective-permute-start | bytes 811016 | tf_op jit(solution)/shard_map/ppermute | solution.py:296
  35.6 13.4 %collective-permute-start.7 = (bf16[528,256]{1,0:T(8,128)(2,1)S(1)}, bf16[528,256]{1,0:T(8,128)(2,1)S(1)}, u32[]{:S(2)}, u32[]{:S(2)}) collective-permute-start(bf16[528,256]{1,0:T(8,128)(2,1)S(1)} %get-tuple-element.19.refs_0_), channel_id=1, source_target_pairs={{0,16},{16,32},{32,48},{48,64},{64,80},{80,96},{96,112},{112,0},{1... | collective-permute-start | bytes 811016 | tf_op jit(solution)/shard_map/ppermute | solution.py:296
  40.8 11.5 %collective-permute-start.3 = (bf16[528,256]{1,0:T(8,128)(2,1)S(1)}, bf16[528,256]{1,0:T(8,128)(2,1)S(1)}, u32[]{:S(2)}, u32[]{:S(2)}) collective-permute-start(bf16[528,256]{1,0:T(8,128)(2,1)S(1)} %collective-permute-done.1.refs_1_), channel_id=1, source_target_pairs={{0,16},{16,32},{32,48},{48,64},{64,80},{80,96},{96,112},{112,0},{1... | collective-permute-start | bytes 811016 | tf_op jit(solution)/shard_map/ppermute | solution.py:296
  40.8 11.5 %collective-permute-start.10 = (bf16[528,256]{1,0:T(8,128)(2,1)S(1)}, bf16[528,256]{1,0:T(8,128)(2,1)S(1)}, u32[]{:S(2)}, u32[]{:S(2)}) collective-permute-start(bf16[528,256]{1,0:T(8,128)(2,1)S(1)} %collective-permute-done.8.refs_2_), channel_id=1, source_target_pairs={{0,112},{16,0},{32,16},{48,32},{64,48},{80,64},{96,80},{112,96},{1... | collective-permute-start | bytes 811016 | tf_op jit(solution)/shard_map/ppermute | solution.py:296
  45.5 11.6 %collective-permute-start.4 = (bf16[528,256]{1,0:T(8,128)(2,1)S(1)}, bf16[528,256]{1,0:T(8,128)(2,1)S(1)}, u32[]{:S(2)}, u32[]{:S(2)}) collective-permute-start(bf16[528,256]{1,0:T(8,128)(2,1)S(1)} %collective-permute-done.2.refs_2_), channel_id=1, source_target_pairs={{0,112},{16,0},{32,16},{48,32},{64,48},{80,64},{96,80},{112,96},{1... | collective-permute-start | bytes 811016 | tf_op jit(solution)/shard_map/ppermute | solution.py:296
  49.0 11.5 %collective-permute-start.9 = (bf16[528,256]{1,0:T(8,128)(2,1)S(1)}, bf16[528,256]{1,0:T(8,128)(2,1)S(1)}, u32[]{:S(2)}, u32[]{:S(2)}) collective-permute-start(bf16[528,256]{1,0:T(8,128)(2,1)S(1)} %collective-permute-done.7.refs_1_), channel_id=1, source_target_pairs={{0,16},{16,32},{32,48},{48,64},{64,80},{80,96},{96,112},{112,0},{1... | collective-permute-start | bytes 811016 | tf_op jit(solution)/shard_map/ppermute | solution.py:296
  52.2 9.7 %collective-permute-start.5 = (bf16[528,256]{1,0:T(8,128)(2,1)S(1)}, bf16[528,256]{1,0:T(8,128)(2,1)}, u32[]{:S(2)}, u32[]{:S(2)}) collective-permute-start(bf16[528,256]{1,0:T(8,128)(2,1)S(1)} %collective-permute-done.3.refs_3_), channel_id=1, source_target_pairs={{0,16},{16,32},{32,48},{48,64},{64,80},{80,96},{96,112},{112,0},{1... | collective-permute-start | bytes 811016 | tf_op jit(solution)/shard_map/ppermute | solution.py:296
  52.2 10.6 %collective-permute-start.12 = (bf16[528,256]{1,0:T(8,128)(2,1)S(1)}, bf16[528,256]{1,0:T(8,128)(2,1)}, u32[]{:S(2)}, u32[]{:S(2)}) collective-permute-start(bf16[528,256]{1,0:T(8,128)(2,1)S(1)} %collective-permute-done.10.refs_4_), channel_id=1, source_target_pairs={{0,112},{16,0},{32,16},{48,32},{64,48},{80,64},{96,80},{112,96},{1... | collective-permute-start | bytes 811016 | tf_op jit(solution)/shard_map/ppermute | solution.py:296
  57.1 11.6 %collective-permute-start.6 = (bf16[528,256]{1,0:T(8,128)(2,1)S(1)}, bf16[528,256]{1,0:T(8,128)(2,1)}, u32[]{:S(2)}, u32[]{:S(2)}) collective-permute-start(bf16[528,256]{1,0:T(8,128)(2,1)S(1)} %collective-permute-done.4.refs_4_), channel_id=1, source_target_pairs={{0,112},{16,0},{32,16},{48,32},{64,48},{80,64},{96,80},{112,96},{1... | collective-permute-start | bytes 811016 | tf_op jit(solution)/shard_map/ppermute | solution.py:296
  60.5 13.9 %collective-permute-start.11 = (bf16[528,256]{1,0:T(8,128)(2,1)S(1)}, bf16[528,256]{1,0:T(8,128)(2,1)}, u32[]{:S(2)}, u32[]{:S(2)}) collective-permute-start(bf16[528,256]{1,0:T(8,128)(2,1)S(1)} %collective-permute-done.9.refs_3_), channel_id=1, source_target_pairs={{0,16},{16,32},{32,48},{48,64},{64,80},{80,96},{96,112},{112,0},{1... | collective-permute-start | bytes 811016 | tf_op jit(solution)/shard_map/ppermute | solution.py:296
  62.0 17.6 %collective-permute-start.13 = (bf16[528,256]{1,0:T(8,128)(2,1)}, bf16[528,256]{1,0:T(8,128)(2,1)S(1)}, u32[]{:S(2)}, u32[]{:S(2)}) collective-permute-start(bf16[528,256]{1,0:T(8,128)(2,1)} %collective-permute-done.5.refs_5_), channel_id=1, source_target_pairs={{0,16},{16,32},{32,48},{48,64},{64,80},{80,96},{96,112},{112,0},{1... | collective-permute-start | bytes 811016 | tf_op jit(solution)/shard_map/ppermute | solution.py:296
  62.9 16.8 %collective-permute-start.14 = (bf16[528,256]{1,0:T(8,128)(2,1)}, bf16[528,256]{1,0:T(8,128)(2,1)S(1)}, u32[]{:S(2)}, u32[]{:S(2)}) collective-permute-start(bf16[528,256]{1,0:T(8,128)(2,1)} %collective-permute-done.12.refs_6_), channel_id=1, source_target_pairs={{0,112},{16,0},{32,16},{48,32},{64,48},{80,64},{96,80},{112,96},{1... | collective-permute-start | bytes 811016 | tf_op jit(solution)/shard_map/ppermute | solution.py:296
